TPU v7x, 512 devices: a whole 4x8x8 slice. The times are simulated.
512 devices in a mesh: seq: 16 (over y_lo, z), res: 32 (over x, y_hi, core).
Axes of the slice: x: 4, y: 8 (y_hi: 4, y_lo: 2; y = y_hi * 2 + y_lo), z: 8, core: 2. Of those that a mesh axis runs over, the one named last changes fastest.
Arguments:
- activations: bfloat16 [1024, 128, 768], P('seq', 'res'), may hold values from -10 to 10
- out_grad: bfloat16 [1024, 128, 768], P('seq', 'res'), may hold values from -96 to 96
- w_query: bfloat16 [768, 512], replicated, may hold values from -0.14433757 to 0.14433757
- w_key: bfloat16 [768, 512], replicated, may hold values from -0.14433757 to 0.14433757
- w_value: bfloat16 [768, 512], replicated, may hold values from -0.21875 to 0.21875
- w_output: bfloat16 [512, 768], replicated, may hold values from -0.25 to 0.25
Outputs:
- input_grad: bfloat16 [1024, 128, 768], P('seq', 'res')
All inputs are finite; a program needn't handle non-finite values.
Results may differ from a plain program's by a relative error of at most 0.0085.
Values may be sent and summed in bfloat16 or wider, within the bound.
A program may use at most 64 MiB of HBM per device.

v0:
```python
import math

import jax
import jax.numpy as jnp
from jax import lax
from jax.sharding import PartitionSpec as P

HEADS = 8
HEAD_DIM = 64


def project(block, weight):
    leading = block.shape[:-1]
    flat = block.reshape(-1, block.shape[-1])
    result = jnp.dot(flat, weight, preferred_element_type=jnp.float32).astype(jnp.bfloat16)
    return result.reshape(leading + (weight.shape[1],))


def back_project(query_grad, key_grad, value_grad, w_query, w_key, w_value):
    leading = query_grad.shape[:-1]
    feature = query_grad.shape[-1]
    total = jnp.dot(query_grad.reshape(-1, feature), w_query.T, preferred_element_type=jnp.float32)
    total = total + jnp.dot(
        key_grad.reshape(-1, feature), w_key.T, preferred_element_type=jnp.float32
    )
    total = total + jnp.dot(
        value_grad.reshape(-1, feature), w_value.T, preferred_element_type=jnp.float32
    )
    return total.astype(jnp.bfloat16).reshape(leading + (w_query.shape[0],))


def body(activations, out_grad, w_query, w_key, w_value, w_output):
    seqs_total = activations.shape[0] * lax.axis_size("seq")
    score_scale = 1.0 / math.sqrt(HEAD_DIM * seqs_total)
    queries = project(activations, w_query)
    key_rows = project(activations, w_key)
    values = project(activations, w_value)
    head_grad = project(out_grad, w_output.T)
    queries, key_rows, values, head_grad = (
        lax.all_to_all(queries, "res", split_axis=0, concat_axis=1, tiled=True),
        lax.all_to_all(key_rows, "res", split_axis=0, concat_axis=1, tiled=True),
        lax.all_to_all(values, "res", split_axis=0, concat_axis=1, tiled=True),
        lax.all_to_all(head_grad, "res", split_axis=0, concat_axis=1, tiled=True),
    )
    local_seqs = queries.shape[0]
    length = queries.shape[1]
    query_heads = queries.reshape(local_seqs, length, HEADS, HEAD_DIM)
    key_heads = key_rows.reshape(local_seqs, length, HEADS, HEAD_DIM)
    value_heads = values.reshape(local_seqs, length, HEADS, HEAD_DIM)
    grad_heads = head_grad.reshape(local_seqs, length, HEADS, HEAD_DIM)
    score_part = jnp.einsum(
        "sihe,sjhe->hij", query_heads, key_heads, preferred_element_type=jnp.float32
    )
    scores = score_scale * lax.psum(score_part, ("seq", "res"))
    prob_part = jnp.einsum(
        "sihe,sjhe->hij", grad_heads, value_heads, preferred_element_type=jnp.float32
    )
    probability = jax.nn.softmax(scores, axis=-1)
    prob_grad = lax.psum(prob_part, ("seq", "res"))
    row_total = jnp.sum(probability * prob_grad, axis=-1, keepdims=True)
    score_grad = (score_scale * probability * (prob_grad - row_total)).astype(jnp.bfloat16)
    prob_low = probability.astype(jnp.bfloat16)
    query_grad = (
        jnp.einsum("hij,sjhe->sihe", score_grad, key_heads, preferred_element_type=jnp.float32)
        .astype(jnp.bfloat16)
        .reshape(local_seqs, length, -1)
    )
    key_grad = (
        jnp.einsum("hij,sihe->sjhe", score_grad, query_heads, preferred_element_type=jnp.float32)
        .astype(jnp.bfloat16)
        .reshape(local_seqs, length, -1)
    )
    value_grad = (
        jnp.einsum("hij,sihe->sjhe", prob_low, grad_heads, preferred_element_type=jnp.float32)
        .astype(jnp.bfloat16)
        .reshape(local_seqs, length, -1)
    )
    query_back, key_back, value_back = (
        lax.all_to_all(query_grad, "res", split_axis=1, concat_axis=0, tiled=True),
        lax.all_to_all(key_grad, "res", split_axis=1, concat_axis=0, tiled=True),
        lax.all_to_all(value_grad, "res", split_axis=1, concat_axis=0, tiled=True),
    )
    return back_project(query_back, key_back, value_back, w_query, w_key, w_value)


def solution(mesh):
    return jax.shard_map(
        body,
        mesh=mesh,
        in_specs=(P("seq", "res", None), P("seq", "res", None), P(), P(), P(), P()),
        out_specs=P("seq", "res", None),
        check_vma=False,
    )
```

profile of v0, /device:TPU:1, one launch (start us, length us, event | category | flops | bytes accessed | tf_op | source)
XLA Modules:
  0.0 440.0 jit_solution(5027274901850484126)
XLA Ops:
  6.5 1.2 reshape.63
  9.0 11.2 %all-to-all-start.3 = ((bf16[64,4,512]{2,1,0:T(4,128)(2,1)}), bf16[64,4,512]{2,1,0:T(4,128)(2,1)S(1)}, u32[]{:S(2)}, u32[]{:S(2)}) async-start(bf16[64,4,512]{2,1,0:T(4,128)(2,1)} %reshape.71), calls=%async_computation.3 | async-start | bytes 524288 | tf_op jit(solution)/shard_map/all_to_all | solution.py:42
  21.4 11.9 %all-to-all-done.3 = bf16[64,4,512]{2,1,0:T(4,128)(2,1)S(1)} async-done(((bf16[64,4,512]{2,1,0:T(4,128)(2,1)}), bf16[64,4,512]{2,1,0:T(4,128)(2,1)S(1)}, u32[]{:S(2)}, u32[]{:S(2)}) %all-to-all-start.3) | async-done | bytes 262176 | tf_op jit(solution)/shard_map/all_to_all | solution.py:42
  33.3 4.3 all-to-all-start.1
  37.6 1.1 convolution_convert_fusion.6
  38.7 1.7 reshape.64
  40.4 10.2 %all-to-all-done.1 = bf16[64,4,512]{2,1,0:T(4,128)(2,1)S(1)} async-done(((bf16[64,4,512]{2,1,0:T(4,128)(2,1)}), bf16[64,4,512]{2,1,0:T(4,128)(2,1)S(1)}, u32[]{:S(2)}, u32[]{:S(2)}) %all-to-all-start.1) | async-done | bytes 262176 | tf_op jit(solution)/shard_map/all_to_all | solution.py:40
  51.3 4.6 %all-to-all-start = ((bf16[64,4,512]{2,1,0:T(4,128)(2,1)}), bf16[64,4,512]{2,1,0:T(4,128)(2,1)}, u32[]{:S(2)}, u32[]{:S(2)}) async-start(bf16[64,4,512]{2,1,0:T(4,128)(2,1)} %reshape.64), calls=%async_computation | async-start | bytes 524288 | tf_op jit(solution)/shard_map/all_to_all | solution.py:41
  55.9 1.1 reshape.68
  57.0 1.5 convolution_convert_fusion.4
  59.3 9.5 %all-to-all-done = bf16[64,4,512]{2,1,0:T(4,128)(2,1)} async-done(((bf16[64,4,512]{2,1,0:T(4,128)(2,1)}), bf16[64,4,512]{2,1,0:T(4,128)(2,1)}, u32[]{:S(2)}, u32[]{:S(2)}) %all-to-all-start) | async-done | bytes 262176 | tf_op jit(solution)/shard_map/all_to_all | solution.py:41
  68.8 4.6 %all-to-all-start.2 = ((bf16[64,4,512]{2,1,0:T(4,128)(2,1)}), bf16[64,4,512]{2,1,0:T(4,128)(2,1)}, u32[]{:S(2)}, u32[]{:S(2)}) async-start(bf16[64,4,512]{2,1,0:T(4,128)(2,1)} %reshape.69), calls=%async_computation.2 | async-start | bytes 524288 | tf_op jit(solution)/shard_map/all_to_all | solution.py:43
  75.3 1.7 copy.40
  77.0 1.3 reshape.65
  78.3 1.0 copy.48
  79.3 1.3 reshape.67
  81.6 4.6 %all-to-all-done.2 = bf16[64,4,512]{2,1,0:T(4,128)(2,1)} async-done(((bf16[64,4,512]{2,1,0:T(4,128)(2,1)}), bf16[64,4,512]{2,1,0:T(4,128)(2,1)}, u32[]{:S(2)}, u32[]{:S(2)}) %all-to-all-start.2) | async-done | bytes 262176 | tf_op jit(solution)/shard_map/all_to_all | solution.py:43
  86.3 1.7 copy.44
  88.0 1.3 reshape.70
  90.3 2.2 convolution_bitcast_fusion
  92.5 1.1 convolution_bitcast_fusion.1
  93.6 272.5 %all-reduce.3.cloned.1.call-done = (f32[8,128,128]{2,1,0:T(8,128)}, f32[8,128,128]{2,1,0:T(8,128)}) async-done(((f32[8,128,128]{2,1,0:T(8,128)}, f32[8,128,128]{2,1,0:T(8,128)}), (f32[8,128,128]{2,1,0:T(8,128)}, f32[8,128,128]{2,1,0:T(8,128)})) %all-reduce.3.cloned.1.call-update) | async-done | bytes 1048592 | tf_op jit(solution)/shard_map/psum | solution.py:59
  366.2 2.2 fusion.34
  368.3 2.9 fusion.10
  372.2 8.3 %all-to-all-start.6 = ((bf16[2,128,512]{2,0,1:T(2,128)(2,1)}), bf16[2,128,512]{2,0,1:T(2,128)(2,1)S(1)}, u32[]{:S(2)}, u32[]{:S(2)}) async-start(bf16[2,128,512]{2,0,1:T(2,128)(2,1)} %copy.58), calls=%async_computation.6 | async-start | bytes 524288 | tf_op jit(solution)/shard_map/all_to_all | solution.py:81
  380.5 7.6 %fusion.8 = bf16[2,128,8,64]{1,3,0,2:T(8,128)(2,1)} fusion(bf16[2,128,8,64]{1,3,0,2:T(8,128)(2,1)S(1)} %copy-done.5, f32[8,128,128]{2,1,0:T(8,128)} %get-tuple-element.5, f32[8,128,128]{2,1,0:T(8,128)} %get-tuple-element.8, f32[8,128]{1,0:T(8,128)S(1)} %get-tuple-element.7), kind=kOutput, calls=%fused_computation.19 | convolution fusion | flops 34604160 | bytes 1576960 | tf_op jit(solution)/shard_map/hij,sjhe->sihe/dot_general | solution.py:64
  390.0 4.0 all-to-all-done.6
  394.0 5.8 %all-to-all-start.4 = ((bf16[2,128,512]{2,0,1:T(2,128)(2,1)}), bf16[2,128,512]{2,0,1:T(2,128)(2,1)S(1)}, u32[]{:S(2)}, u32[]{:S(2)}) async-start(bf16[2,128,512]{2,0,1:T(2,128)(2,1)} %copy.50), calls=%async_computation.4 | async-start | bytes 524288 | tf_op jit(solution)/shard_map/all_to_all | solution.py:79
  399.8 6.9 %fusion.9 = bf16[2,128,8,64]{1,3,0,2:T(8,128)(2,1)S(1)} fusion(bf16[2,128,8,64]{1,3,0,2:T(8,128)(2,1)S(1)} %copy-done.4, f32[8,128,128]{2,1,0:T(8,128)} %get-tuple-element.5, f32[8,128,128]{2,1,0:T(8,128)} %get-tuple-element.8, f32[8,128]{1,0:T(8,128)S(1)} %get-tuple-element.7), kind=kOutput, calls=%fused_computation.20 | convolution fusion | flops 34604160 | bytes 1576960 | tf_op jit(solution)/shard_map/hij,sihe->sjhe/dot_general | solution.py:69
  407.6 5.7 %all-to-all-done.4 = bf16[2,128,512]{2,0,1:T(2,128)(2,1)S(1)} async-done(((bf16[2,128,512]{2,0,1:T(2,128)(2,1)}), bf16[2,128,512]{2,0,1:T(2,128)(2,1)S(1)}, u32[]{:S(2)}, u32[]{:S(2)}) %all-to-all-start.4) | async-done | bytes 262176 | tf_op jit(solution)/shard_map/all_to_all | solution.py:79
  413.3 4.1 all-to-all-start.5
  417.8 13.1 %all-to-all-done.5 = bf16[2,128,512]{2,0,1:T(2,128)(2,1)S(1)} async-done(((bf16[2,128,512]{2,0,1:T(2,128)(2,1)}), bf16[2,128,512]{2,0,1:T(2,128)(2,1)S(1)}, u32[]{:S(2)}, u32[]{:S(2)}) %all-to-all-start.5) | async-done | bytes 262176 | tf_op jit(solution)/shard_map/all_to_all | solution.py:80
  (44 shorter events, 14.0 us)
Async XLA Ops:
  6.5 13.7 %copy-start = (bf16[768,512]{1,0:T(8,128)(2,1)S(1)}, bf16[768,512]{1,0:T(8,128)(2,1)}, u32[]{:S(2)}) copy-start(bf16[768,512]{1,0:T(8,128)(2,1)} %param.8) | copy-start | bytes 2359300
  6.5 1.3 copy-start.1
  9.0 24.3 %all-to-all-start.3 = ((bf16[64,4,512]{2,1,0:T(4,128)(2,1)}), bf16[64,4,512]{2,1,0:T(4,128)(2,1)S(1)}, u32[]{:S(2)}, u32[]{:S(2)}) async-start(bf16[64,4,512]{2,1,0:T(4,128)(2,1)} %reshape.71), calls=%async_computation.3 | async-start | bytes 524288 | tf_op jit(solution)/shard_map/all_to_all | solution.py:42
  20.6 17.0 %copy-start.2 = (bf16[768,512]{1,0:T(8,128)(2,1)S(1)}, bf16[768,512]{1,0:T(8,128)(2,1)}, u32[]{:S(2)}) copy-start(bf16[768,512]{1,0:T(8,128)(2,1)} %param.9) | copy-start | bytes 2359300
  33.3 17.3 %all-to-all-start.1 = ((bf16[64,4,512]{2,1,0:T(4,128)(2,1)}), bf16[64,4,512]{2,1,0:T(4,128)(2,1)S(1)}, u32[]{:S(2)}, u32[]{:S(2)}) async-start(bf16[64,4,512]{2,1,0:T(4,128)(2,1)} %reshape.66), calls=%async_computation.1 | async-start | bytes 524288 | tf_op jit(solution)/shard_map/all_to_all | solution.py:40
  50.6 0.7 copy-start.6
  51.3 17.5 %all-to-all-start = ((bf16[64,4,512]{2,1,0:T(4,128)(2,1)}), bf16[64,4,512]{2,1,0:T(4,128)(2,1)}, u32[]{:S(2)}, u32[]{:S(2)}) async-start(bf16[64,4,512]{2,1,0:T(4,128)(2,1)} %reshape.64), calls=%async_computation | async-start | bytes 524288 | tf_op jit(solution)/shard_map/all_to_all | solution.py:41
  68.8 17.5 %all-to-all-start.2 = ((bf16[64,4,512]{2,1,0:T(4,128)(2,1)}), bf16[64,4,512]{2,1,0:T(4,128)(2,1)}, u32[]{:S(2)}, u32[]{:S(2)}) async-start(bf16[64,4,512]{2,1,0:T(4,128)(2,1)} %reshape.69), calls=%async_computation.2 | async-start | bytes 524288 | tf_op jit(solution)/shard_map/all_to_all | solution.py:43
  73.4 292.8 %all-reduce.3.cloned.1.call-start = ((), (), s32[]{:S(2)}) async-start(), calls=%async_computation.7 | async-start | bytes 2097152 | tf_op jit(solution)/shard_map/psum | solution.py:59
  73.6 1.0 copy-start.7
  90.3 2.2 copy-start.4
  90.3 2.2 copy-start.5
  366.2 2.2 copy-start.3
  372.2 21.8 %all-to-all-start.6 = ((bf16[2,128,512]{2,0,1:T(2,128)(2,1)}), bf16[2,128,512]{2,0,1:T(2,128)(2,1)S(1)}, u32[]{:S(2)}, u32[]{:S(2)}) async-start(bf16[2,128,512]{2,0,1:T(2,128)(2,1)} %copy.58), calls=%async_computation.6 | async-start | bytes 524288 | tf_op jit(solution)/shard_map/all_to_all | solution.py:81
  394.0 19.3 %all-to-all-start.4 = ((bf16[2,128,512]{2,0,1:T(2,128)(2,1)}), bf16[2,128,512]{2,0,1:T(2,128)(2,1)S(1)}, u32[]{:S(2)}, u32[]{:S(2)}) async-start(bf16[2,128,512]{2,0,1:T(2,128)(2,1)} %copy.50), calls=%async_computation.4 | async-start | bytes 524288 | tf_op jit(solution)/shard_map/all_to_all | solution.py:79
  413.3 17.6 %all-to-all-start.5 = ((bf16[2,128,512]{2,0,1:T(2,128)(2,1)}), bf16[2,128,512]{2,0,1:T(2,128)(2,1)S(1)}, u32[]{:S(2)}, u32[]{:S(2)}) async-start(bf16[2,128,512]{2,0,1:T(2,128)(2,1)} %copy.54), calls=%async_computation.5 | async-start | bytes 524288 | tf_op jit(solution)/shard_map/all_to_all | solution.py:80
Sparse Core Ops, SparseCore 0:
  93.8 272.3 all-reduce.2
where the time goes:
time: 441 us; the launch traced here: 440 us
  waiting for transfers between devices  332 us (75%)
  starting transfers between devices  43 us (10%)
  matrix products  25.3 us (6%)
  local copies, waits for them, and re-layouts  24.3 us (6%)
  between operations  13.7 us (3%)
    psum x1, waiting for transfers between devices, body(): prob_grad = lax.psum(prob_part, ('seq', 'res'))  273 us
    all_to_all x1, waiting for transfers between devices, body(): lax.all_to_all(key_grad, 'res', split_axis=1, concat_axis=0, tiled=True)  13.1 us
    all_to_all x1, waiting for transfers between devices, body(): lax.all_to_all(values, 'res', split_axis=0, concat_axis=1, tiled=True)  11.9 us
    all_to_all x1, starting transfers between devices, body(): lax.all_to_all(values, 'res', split_axis=0, concat_axis=1, tiled=True)  11.2 us
    all_to_all x1, waiting for transfers between devices, body(): lax.all_to_all(queries, 'res', split_axis=0, concat_axis=1, tiled=True)  10.2 us
    all_to_all x1, waiting for transfers between devices, body(): lax.all_to_all(key_rows, 'res', split_axis=0, concat_axis=1, tiled=True)  9.46 us
  transfers between devices with their start and end apart: 8, of which 8 were waited for; matrix products, arithmetic and copies ran while one was open for 7% of the time, Pallas kernels for 0%

commit v1 on v0

v1 whole, which is shorter than its diff:
```python
import math

import jax
import jax.numpy as jnp
from jax import lax
from jax.sharding import Mesh, PartitionSpec as P

HEADS = 8
HEAD_DIM = 64
GROUP = ("x", "yh", "core")


def project(block, weight):
    rows = block.shape[0] * block.shape[1]
    flat = block.reshape(rows, block.shape[-1])
    return jnp.dot(flat, weight, preferred_element_type=jnp.float32).astype(jnp.bfloat16)


def body(activations, out_grad, w_query, w_key, w_value, w_output):
    seqs, res, _ = activations.shape
    chunk = seqs // 4
    scale = 1.0 / math.sqrt(HEAD_DIM * seqs * lax.axis_size("seq"))

    def spread(block):
        block = block.reshape(4, chunk, res, 4, 2, HEAD_DIM)
        return block.transpose(3, 0, 4, 1, 2, 5).reshape(32, chunk * res, HEAD_DIM)

    queries = spread(project(activations, w_query))
    key_rows = spread(project(activations, w_key))
    values = spread(project(activations, w_value))
    head_grad = spread(project(out_grad, w_output.T))
    packed = jnp.concatenate([queries, key_rows, head_grad, values], axis=-1)
    packed = lax.all_to_all(packed, GROUP, split_axis=0, concat_axis=0, tiled=True)
    packed = packed.reshape(32, chunk, res, 4, HEAD_DIM)
    packed = packed.transpose(3, 1, 0, 2, 4).reshape(4, chunk, 32 * res, HEAD_DIM)
    q, k, g, v = packed[0], packed[1], packed[2], packed[3]
    parts = jnp.stack(
        [
            jnp.einsum("sie,sje->ij", q, k, preferred_element_type=jnp.float32),
            jnp.einsum("sie,sje->ij", g, v, preferred_element_type=jnp.float32),
        ]
    )
    parts = lax.psum(parts, ("seq", "yh"))
    probability = jax.nn.softmax(scale * parts[0], axis=-1)
    prob_grad = parts[1]
    row_total = jnp.sum(probability * prob_grad, axis=-1, keepdims=True)
    score_grad = (scale * probability * (prob_grad - row_total)).astype(jnp.bfloat16)
    prob_low = probability.astype(jnp.bfloat16)
    f32 = jnp.float32
    grads = jnp.stack(
        [
            jnp.einsum("ij,sje->sie", score_grad, k, preferred_element_type=f32),
            jnp.einsum("ij,sie->sje", score_grad, q, preferred_element_type=f32),
            jnp.einsum("ij,sie->sje", prob_low, g, preferred_element_type=f32),
        ]
    ).astype(jnp.bfloat16)
    grads = grads.reshape(3, chunk, 32, res, HEAD_DIM).transpose(2, 1, 3, 0, 4)
    grads = lax.all_to_all(
        grads.reshape(32, chunk * res, 3 * HEAD_DIM), GROUP, split_axis=0, concat_axis=0, tiled=True
    )
    grads = grads.reshape(4, 4, 2, chunk * res, 3, HEAD_DIM).transpose(4, 1, 3, 0, 2, 5)
    grads = grads.reshape(3, seqs * res, HEADS * HEAD_DIM)
    total = jnp.dot(grads[0], w_query.T, preferred_element_type=f32)
    total = total + jnp.dot(grads[1], w_key.T, preferred_element_type=f32)
    total = total + jnp.dot(grads[2], w_value.T, preferred_element_type=f32)
    return total.astype(jnp.bfloat16).reshape(activations.shape)


def solution(mesh):
    fine = Mesh(mesh.devices.reshape(16, 4, 4, 2), ("seq",) + GROUP)
    rows = P("seq", GROUP, None)
    return jax.shard_map(
        body,
        mesh=fine,
        in_specs=(rows, rows, P(), P(), P(), P()),
        out_specs=rows,
        check_vma=False,
    )
```

time: 441 us -> 284 us (0.64)
  waiting for transfers between devices: 332 us -> 147 us
  blocking collectives: 0 us -> 80.5 us
  starting transfers between devices: 43 us -> 0.01 us
  matrix products: 25.3 us -> 9.26 us
    psum x1, waiting for transfers between devices: 273 us -> 147 us  [body(): parts = lax.psum(parts, ('seq', 'yh'))]
    all_to_all x0 -> x2, blocking collectives: none -> 80.5 us  [the longest x1 40.9 us: body(): lax.all_to_all(grads.reshape(32, chunk * res, 3 * HEAD_DIM), GROUP, split...]
    all_to_all x7 -> x0, waiting for transfers between devices: 59 us -> none  [the longest x1 13.1 us: body(): lax.all_to_all(key_grad, 'res', split_axis=1, concat_axis=0, tiled=True)]
    all_to_all x7 -> x0, starting transfers between devices: 42.9 us -> none  [the longest x1 11.2 us: body(): lax.all_to_all(values, 'res', split_axis=0, concat_axis=1, tiled=True)]
    dot_general x8, matrix products: 21.9 us -> 5.49 us  [the longest x1 1.37 us: body(): jnp.einsum('sie,sje->ij', g, v, preferred_element_type=jnp.float32)]
    slice x0 -> x9, local copies, waits for them, and re-layouts: none -> 11.5 us  [the longest x5 8.29 us: body(): q, k, g, v = (packed[0], packed[1], packed[2], packed[3])]
    reshape x20 -> x13, local copies, waits for them, and re-layouts: 17.2 us -> 10.1 us  [the longest x1 3.32 us: body(): packed = packed.reshape(32, chunk, res, 4, HEAD_DIM)]
  transfers between devices with their start and end apart: 8 -> 1, of which waited for: 8 -> 1; matrix products, arithmetic and copies ran while one was open for 7% -> 0% of each run, Pallas kernels for 0% -> 0%
where the time goes in v1:
time: 284 us
  waiting for transfers between devices  147 us (52%)
  blocking collectives  80.5 us (28%)
  local copies, waits for them, and re-layouts  28.5 us (10%)
  between operations  13.8 us (5%)
  matrix products  9.26 us (3%)
  other arithmetic  4.85 us (2%)
    psum x1, waiting for transfers between devices, body(): parts = lax.psum(parts, ('seq', 'yh'))  147 us
    all_to_all x1, blocking collectives, body(): lax.all_to_all(grads.reshape(32, chunk * res, 3 * HEAD_DIM), GROUP, split...  40.9 us
    all_to_all x1, blocking collectives, body(): lax.all_to_all(packed, GROUP, split_axis=0, concat_axis=0, tiled=True)  39.6 us
    slice x5, local copies, waits for them, and re-layouts, body(): q, k, g, v = (packed[0], packed[1], packed[2], packed[3])  8.29 us
  transfers between devices with their start and end apart: 1, of which 1 were waited for; matrix products, arithmetic and copies ran while one was open for 0% of the time, Pallas kernels for 0%

profile of v1, /device:TPU:1, one launch (start us, length us, event | category | flops | bytes accessed | tf_op | source)
XLA Modules:
  0.0 283.7 jit_solution(3735265963943056601)
XLA Ops:
  6.5 1.2 reshape.113
  7.8 1.5 convolution_convert_fusion.3
  11.9 1.5 convolution_convert_fusion.4
  14.0 0.7 pad_maximum_fusion
  14.7 39.6 %all_to_all.10 = bf16[32,64,256]{2,1,0:T(8,128)(2,1)} all-to-all(bf16[32,64,256]{2,1,0:T(8,128)(2,1)S(1)} %pad_maximum_fusion), channel_id=1, replica_groups=mesh['seq'=16,'x'=4,'yh'=4,'core'=2] {'x','yh','core'}, dimensions={0} | all-to-all | bytes 2097152 | tf_op jit(solution)/shard_map/all_to_all | solution.py:33
  54.3 3.3 %reshape.123 = bf16[32,16,4,4,64]{4,3,2,1,0:T(4,128)(2,1)S(1)} reshape(bf16[32,64,256]{2,1,0:T(8,128)(2,1)} %all_to_all.10) | data formatting | bytes 2097152 | tf_op jit(solution)/shard_map/reshape | solution.py:34
  57.6 5.7 %fusion.14 = (bf16[1,16,32,4,64]{4,0,3,1,2:T(2,128)(2,1)S(1)}, bf16[1,16,32,4,64]{4,0,3,1,2:T(2,128)(2,1)}, bf16[1,16,32,4,64]{4,0,3,1,2:T(2,128)(2,1)}, bf16[1,16,32,4,64]{4,0,3,1,2:T(2,128)(2,1)}) fusion(bf16[4,16,32,4,64]{4,0,3,1,2:T(4,128)(2,1)S(1)} %bitcast.78), kind=kLoop, calls=%fused_computation.31 | loop fusion | bytes 2097152 | tf_op jit(solution)/shard_map/slice | solution.py:36
  63.4 1.1 copy.19
  64.6 2.2 copy.16
  67.0 0.5 copy.17
  67.6 0.5 copy.13
  68.1 1.4 convolution_bitcast_fusion
  69.7 0.7 pad_maximum_fusion.1
  70.4 146.7 %all-reduce.2.cloned.1.call-done = f32[2,128,128]{2,1,0:T(8,128)} async-done(((f32[2,128,128]{2,1,0:T(8,128)}), f32[2,128,128]{2,1,0:T(8,128)}) %all-reduce.2.cloned.1.call-update) | async-done | bytes 131088 | tf_op jit(solution)/shard_map/psum | solution.py:43
  217.2 1.0 fusion.8
  218.2 1.0 fusion.7
  219.2 1.1 fusion.5
  220.3 1.2 fusion.1
  221.5 0.4 copy.20
  221.9 1.2 fusion.2
  223.1 0.4 copy.22
  223.9 0.4 copy.24
  224.7 1.5 copy.25
  226.2 2.4 reshape.124
  228.5 40.9 %all_to_all.11 = bf16[32,64,192]{2,1,0:T(8,128)(2,1)S(1)} all-to-all(bf16[32,64,192]{2,1,0:T(8,128)(2,1)} %reshape.124), channel_id=1, replica_groups=mesh['seq'=16,'x'=4,'yh'=4,'core'=2] {'x','yh','core'}, dimensions={0} | all-to-all | bytes 1572864 | tf_op jit(solution)/shard_map/all_to_all | solution.py:58
  269.4 0.9 copy.26
  270.3 1.0 fusion.15
  271.2 1.3 copy.29
  272.9 0.4 copy.28
  273.7 0.4 copy.27
  274.9 0.4 convolution_add_fusion.1
  276.0 0.8 reshape.126
  (42 shorter events, 6.5 us)
Async XLA Ops:
  6.5 3.7 %copy-start = (bf16[768,512]{1,0:T(8,128)(2,1)S(1)}, bf16[768,512]{1,0:T(8,128)(2,1)}, u32[]{:S(2)}) copy-start(bf16[768,512]{1,0:T(8,128)(2,1)} %param.8) | copy-start | bytes 2359300
  6.5 3.3 %copy-start.4 = (bf16[768,512]{1,0:T(8,128)(2,1)S(1)}, bf16[768,512]{1,0:T(8,128)(2,1)}, u32[]{:S(2)}) copy-start(bf16[768,512]{1,0:T(8,128)(2,1)} %param.9) | copy-start | bytes 2359300
  6.5 210.6 %all-reduce.2.cloned.1.call-start = ((), (), s32[]{:S(2)}) async-start(), calls=%async_computation.2 | async-start | bytes 262144 | tf_op jit(solution)/shard_map/psum | solution.py:43
  10.6 1.2 copy-start.8
  63.3 3.5 %copy-start.2 = (bf16[1,16,32,4,64]{4,0,3,1,2:T(2,128)(2,1)S(1)}, bf16[1,16,32,4,64]{4,0,3,1,2:T(2,128)(2,1)}, u32[]{:S(2)}) copy-start(bf16[1,16,32,4,64]{4,0,3,1,2:T(2,128)(2,1)} %get-tuple-element.7) | copy-start | bytes 786436
  64.6 2.9 %copy-start.1 = (bf16[1,16,32,4,64]{4,0,3,1,2:T(2,128)(2,1)S(1)}, bf16[1,16,32,4,64]{4,0,3,1,2:T(2,128)(2,1)}, u32[]{:S(2)}) copy-start(bf16[1,16,32,4,64]{4,0,3,1,2:T(2,128)(2,1)} %get-tuple-element.8) | copy-start | bytes 786436
  67.0 2.5 copy-start.6
  217.2 6.4 %copy-start.7 = (f32[2,128,128]{2,1,0:T(8,128)S(1)}, f32[2,128,128]{2,1,0:T(8,128)}, u32[]{:S(2)}) copy-start(f32[2,128,128]{2,1,0:T(8,128)} %all-reduce.2.cloned.1.call-done) | copy-start | bytes 393220
  273.4 1.5 copy-start.5
  274.5 1.1 copy-start.3
Sparse Core Ops, SparseCore 0:
  70.5 146.5 all-reduce.1

commit v2 on v1

v2 whole, which is shorter than its diff:
```python
import math

import jax
import jax.numpy as jnp
from jax import lax
from jax.experimental import pallas as pl
from jax.experimental.pallas import tpu as pltpu
from jax.sharding import PartitionSpec as P

MESH = pl.DeviceIdType.MESH
F32, BF16 = jnp.float32, jnp.bfloat16
D = 768
FEATURES = 512
HEAD_DIM = 64
SEQ_RUN = 16
RES = 4
ROWS = SEQ_RUN * RES
NT = (((1,), (1,)), ((), ()))
TN = (((0,), (0,)), ((), ()))


def rows_dot(a, b, dims=(((1,), (0,)), ((), ()))):
    return lax.dot_general(a, b, dims, preferred_element_type=F32)


def kernel(
    scale,
    act, og, wq_hbm, wk_hbm, wv_hbm, wo_hbm,
    out,
    wq, wk, wv, wo, og_v, xr, g_send, gr, v_roll,
    qk_send, gv_send, qk_recv, gv_recv,
    wide, z_qk, z_gv, rolled, masked,
    part, part_recv, total, total_recv, probs,
    wide_v, back_send, back_recv, out_send,
    load_sem, x_send_sem, x_recv_sem, g_send_sem, g_recv_sem,
    qk_send_sem, qk_recv_sem, gv_send_sem, gv_recv_sem, own_sem,
    part_send_sem, part_recv_sem, total_send_sem, total_recv_sem,
    probs_send_sem, probs_recv_sem, back_send_sem, back_recv_sem, back_own_sem,
    out_send_sem, out_recv_sem, out_own_sem,
):
    seq, res = lax.axis_index("seq"), lax.axis_index("res")
    ylo, z = seq // 8, seq % 8
    x, yh, core = res // 8, (res // 2) % 4, res % 2
    g = x * 2 + core
    w = yh * 2 + ylo

    def y_peer(h):
        return (seq, x * 8 + h * 2 + core)

    def head_peer(h):
        return (seq, (h // 2) * 8 + yh * 2 + h % 2)

    def z_peer(k):
        return (ylo * 8 + k, res)

    def line_peer(k):
        return ((k % 2) * 8 + z, x * 8 + (k // 2) * 2 + core)

    def run(h):
        return pl.ds(pl.multiple_of(h * SEQ_RUN, SEQ_RUN), SEQ_RUN)

    loads = [
        pltpu.make_async_copy(og, og_v, load_sem.at[0]),
        pltpu.make_async_copy(wo_hbm, wo, load_sem.at[1]),
        pltpu.make_async_copy(act.at[run(yh)], xr.at[yh], load_sem.at[2]),
        pltpu.make_async_copy(wq_hbm, wq, load_sem.at[3]),
        pltpu.make_async_copy(wk_hbm, wk, load_sem.at[4]),
        pltpu.make_async_copy(wv_hbm, wv, load_sem.at[5]),
    ]
    for load in loads:
        load.start()

    barrier = pltpu.get_barrier_semaphore()

    def greet(k, _):
        pl.semaphore_signal(barrier, inc=1, device_id=head_peer((g + k) % 8), device_id_type=MESH)
        pl.semaphore_signal(barrier, inc=1, device_id=z_peer((z + k) % 8), device_id_type=MESH)
        pl.semaphore_signal(barrier, inc=1, device_id=line_peer((w + k) % 8), device_id_type=MESH)
        return 0

    lax.fori_loop(1, 8, greet, 0)
    pl.semaphore_wait(barrier, 21)

    def x_copy(to, slot):
        return pltpu.make_async_remote_copy(
            act.at[run(to)], xr.at[slot], x_send_sem, x_recv_sem.at[slot],
            device_id=y_peer(to), device_id_type=MESH,
        )

    def g_copy(to, slot):
        return pltpu.make_async_remote_copy(
            g_send.at[to], gr.at[slot], g_send_sem, g_recv_sem.at[slot],
            device_id=y_peer(to), device_id_type=MESH,
        )

    def near_first(k):
        return k + k // 2 - 2 * (k // 3)

    def send_x(k, _):
        x_copy((yh + near_first(k)) % 4, yh).start()
        return 0

    lax.fori_loop(1, 4, send_x, 0)

    loads[0].wait()
    loads[1].wait()
    grad_rows = rows_dot(og_v[...].reshape(4 * ROWS, D), wo[...], NT).astype(BF16)
    g_send[...] = grad_rows.reshape(4, ROWS, FEATURES)

    def send_g(k, _):
        g_copy((yh + near_first(k)) % 4, yh).start()
        return 0

    lax.fori_loop(1, 4, send_g, 0)
    gr[yh] = g_send[yh]

    low_half = lax.broadcasted_iota(jnp.int32, (ROWS, 128), 1) < HEAD_DIM

    def pack(first, second, send, src):
        for p in range(4):
            a, b = first[:, p * 128 : p * 128 + 128], second[:, p * 128 : p * 128 + 128]
            send[2 * p, src] = jnp.where(low_half, a, b)
            send[2 * p + 1, src] = jnp.where(low_half, b, a)

    def spread(send, recv, send_sem, recv_sem, src, own_at):
        def one(k, _):
            to = (g + k) % 8
            pltpu.make_async_remote_copy(
                send.at[to, src], recv.at[g, src], send_sem, recv_sem,
                device_id=head_peer(to), device_id_type=MESH,
            ).start()
            return 0

        lax.fori_loop(1, 8, one, 0)
        pltpu.make_async_copy(send.at[g, src], recv.at[g, src], own_sem.at[own_at, src]).start()

    def roll_pairs(a):
        return jnp.concatenate(
            [pltpu.roll(a[:, p * 128 : p * 128 + 128], HEAD_DIM, 1) for p in range(4)], axis=1
        )

    def do_qk(src):
        rows = xr[src].reshape(ROWS, D)
        q = rows_dot(rows, wq[...]).astype(BF16)
        k = rows_dot(rows, wk[...]).astype(BF16)
        pack(q, roll_pairs(k), qk_send, src)
        spread(qk_send, qk_recv, qk_send_sem, qk_recv_sem, src, 0)
        v_roll[src] = roll_pairs(rows_dot(rows, wv[...]).astype(BF16))

    def do_gv(src):
        pack(gr[src], v_roll[src], gv_send, src)
        spread(gv_send, gv_recv, gv_send_sem, gv_recv_sem, src, 1)

    for load in loads[2:]:
        load.wait()
    do_qk(yh)
    do_gv(yh)

    def next_qk(k, _):
        src = (yh + near_first(k)) % 4
        x_copy(src, src).wait_recv()
        do_qk(src)
        return 0

    lax.fori_loop(1, 4, next_qk, 0)

    def next_gv(k, _):
        src = (yh + near_first(k)) % 4
        g_copy(src, src).wait_recv()
        do_gv(src)
        return 0

    lax.fori_loop(1, 4, next_gv, 0)

    lane = lax.broadcasted_iota(jnp.int32, (128, 128), 1)
    first = (lane // HEAD_DIM) == core
    first_scale = jnp.where(first, 1.0, 0.0).astype(BF16)

    def wait_all(send, recv, recv_sem, own_at):
        part_of = recv.at[pl.ds(0, 7)]
        pltpu.make_async_copy(part_of, part_of, recv_sem).wait()
        for src in range(4):
            pltpu.make_async_copy(send.at[g, src], recv.at[g, src], own_sem.at[own_at, src]).wait()

    def product(recv, keep):
        wide[...] = recv[...].reshape(32 * ROWS, 128).astype(F32)
        for s in range(SEQ_RUN):
            block = jnp.concatenate(
                [wide[pl.ds(s * RES + r, 32, stride=ROWS), :] for r in range(RES)], axis=0
            ).astype(BF16)
            lanes = slice(s * 128, s * 128 + 128)
            keep[:, lanes] = block
            masked[:, lanes] = block * first_scale
            rolled[:, lanes] = pltpu.roll(block, HEAD_DIM, 1)
        return rows_dot(masked[...], rolled[...], NT)

    wait_all(qk_send, qk_recv, qk_recv_sem, 0)
    part[:, 0] = product(qk_recv, z_qk).reshape(8, 16, 128)
    wait_all(gv_send, gv_recv, gv_recv_sem, 1)
    part[:, 1] = product(gv_recv, z_gv).reshape(8, 16, 128)

    def send_part(k, _):
        to = (z + k) % 8
        pltpu.make_async_remote_copy(
            part.at[to], part_recv.at[z], part_send_sem, part_recv_sem,
            device_id=z_peer(to), device_id_type=MESH,
        ).start()
        return 0

    lax.fori_loop(1, 8, send_part, 0)
    part_recv[z] = part[z]
    seven = part_recv.at[pl.ds(0, 7)]
    pltpu.make_async_copy(seven, seven, part_recv_sem).wait()
    total[...] = jnp.sum(part_recv[...], axis=0)

    def send_total(k, _):
        to = (w + k) % 8
        pltpu.make_async_remote_copy(
            total, total_recv.at[w], total_send_sem, total_recv_sem,
            device_id=line_peer(to), device_id_type=MESH,
        ).start()
        return 0

    lax.fori_loop(1, 8, send_total, 0)
    total_recv[w] = total[...]
    seven_t = total_recv.at[pl.ds(0, 7)]
    pltpu.make_async_copy(seven_t, seven_t, total_recv_sem).wait()
    sums = jnp.sum(total_recv[...], axis=0)
    scores, prob_grad = scale * sums[0], sums[1]
    grown = jnp.exp(scores - jnp.max(scores, axis=-1, keepdims=True))
    probability = grown / jnp.sum(grown, axis=-1, keepdims=True)
    row_total = jnp.sum(probability * prob_grad, axis=-1, keepdims=True)
    probs[z, 0] = (scale * probability * (prob_grad - row_total)).astype(BF16)
    probs[z, 1] = probability.astype(BF16)

    def send_probs(k, _):
        to = (z + k) % 8
        pltpu.make_async_remote_copy(
            probs.at[z], probs.at[z], probs_send_sem, probs_recv_sem,
            device_id=z_peer(to), device_id_type=MESH,
        ).start()
        return 0

    lax.fori_loop(1, 8, send_probs, 0)
    seven_p = probs.at[pl.ds(0, 7)]
    pltpu.make_async_copy(seven_p, seven_p, probs_recv_sem).wait()
    score_grad = probs[:, 0].reshape(128, 128)
    prob_low = probs[:, 1].reshape(128, 128)

    to_query = rows_dot(score_grad, z_qk[...])
    to_key = rows_dot(score_grad, z_qk[...], TN)
    to_value = rows_dot(prob_low, z_gv[...], TN)
    for s in range(SEQ_RUN):
        lanes = slice(s * 128, s * 128 + 128)
        block = jnp.where(first, to_key[:, lanes], to_query[:, lanes])
        for r in range(RES):
            wide[pl.ds(s * RES + r, 32, stride=ROWS), :] = block[r * 32 : r * 32 + 32]
    half = SEQ_RUN // 2
    for s in range(half):
        near, far = to_value[:, s * 128 : s * 128 + 128], to_value[:, (s + half) * 128 : (s + half + 1) * 128]
        block = jnp.where(first, near, pltpu.roll(far, HEAD_DIM, 1))
        for r in range(RES):
            wide_v[pl.ds(s * RES + r, 32, stride=ROWS // 2), :] = block[r * 32 : r * 32 + 32]
    back_send[:, :, :ROWS] = wide[...].astype(BF16).reshape(8, 4, ROWS, 128)
    back_send[:, :, ROWS:] = wide_v[...].astype(BF16).reshape(8, 4, ROWS // 2, 128)

    def far_first(k):
        return near_first(3 - k)

    def send_back(k, _):
        src = (yh + far_first(k)) % 4

        def one(j, _):
            to = (g + j) % 8
            pltpu.make_async_remote_copy(
                back_send.at[to, src], back_recv.at[g, src], back_send_sem, back_recv_sem.at[src],
                device_id=head_peer(to), device_id_type=MESH,
            ).start()
            return 0

        lax.fori_loop(1, 8, one, 0)
        pltpu.make_async_copy(back_send.at[g, src], back_recv.at[g, src], back_own_sem.at[src]).start()
        return 0

    lax.fori_loop(0, 4, send_back, 0)

    low_back = lax.broadcasted_iota(jnp.int32, (ROWS + ROWS // 2, 128), 1) < HEAD_DIM

    def out_copy(to, slot):
        return pltpu.make_async_remote_copy(
            out_send.at[to], out.at[run(slot)], out_send_sem, out_recv_sem.at[slot],
            device_id=y_peer(to), device_id_type=MESH,
        )

    def finish(src):
        arrived = back_recv.at[pl.ds(0, 7), src]
        pltpu.make_async_copy(arrived, arrived, back_recv_sem.at[src]).wait()
        pltpu.make_async_copy(back_send.at[g, src], back_recv.at[g, src], back_own_sem.at[src]).wait()
        dq, dk, dv = [], [], []
        for p in range(4):
            a, b = back_recv[2 * p, src], back_recv[2 * p + 1, src]
            straight = jnp.where(low_back, a, b)
            swapped = pltpu.roll(jnp.where(low_back, b, a), HEAD_DIM, 1)
            dk.append(straight[:ROWS])
            dq.append(swapped[:ROWS])
            dv.append(jnp.concatenate([straight[ROWS:], swapped[ROWS:]], axis=0))
        grad = rows_dot(jnp.concatenate(dq, axis=1), wq[...], NT)
        grad = grad + rows_dot(jnp.concatenate(dk, axis=1), wk[...], NT)
        grad = grad + rows_dot(jnp.concatenate(dv, axis=1), wv[...], NT)
        out_send[src] = grad.astype(BF16).reshape(SEQ_RUN, RES, D)

    def finish_far(k, _):
        src = (yh + far_first(k)) % 4
        finish(src)
        out_copy(src, yh).start()
        return 0

    lax.fori_loop(0, 3, finish_far, 0)
    finish(yh)
    own_out = pltpu.make_async_copy(out_send.at[yh], out.at[run(yh)], out_own_sem)
    own_out.start()

    def wait_bytes(ref, sem):
        pltpu.make_async_copy(ref, ref, sem).wait()

    wait_bytes(xr.at[pl.ds(0, 3)], x_send_sem)
    wait_bytes(gr.at[pl.ds(0, 3)], g_send_sem)
    wait_bytes(qk_send.at[pl.ds(0, 7)], qk_send_sem)
    wait_bytes(gv_send.at[pl.ds(0, 7)], gv_send_sem)
    wait_bytes(part_recv.at[pl.ds(0, 7)], part_send_sem)
    wait_bytes(total_recv.at[pl.ds(0, 7)], total_send_sem)
    wait_bytes(probs.at[pl.ds(0, 7)], probs_send_sem)
    wait_bytes(back_send.at[pl.ds(0, 7)], back_send_sem)
    wait_bytes(out_send.at[pl.ds(0, 3)], out_send_sem)

    def wait_out(k, _):
        src = (yh + k) % 4
        out_copy(src, src).wait_recv()
        return 0

    lax.fori_loop(1, 4, wait_out, 0)
    own_out.wait()


def body(activations, out_grad, w_query, w_key, w_value, w_output):
    seqs_total = activations.shape[0] * lax.axis_size("seq")
    scale = 1.0 / math.sqrt(HEAD_DIM * seqs_total)
    any_space = pl.BlockSpec(memory_space=pl.ANY)
    dma = pltpu.SemaphoreType.DMA
    vmem = pltpu.VMEM
    return pl.pallas_call(
        lambda *refs: kernel(scale, *refs),
        out_shape=jax.ShapeDtypeStruct(activations.shape, BF16),
        in_specs=[any_space] * 6,
        out_specs=any_space,
        scratch_shapes=[
            vmem((D, FEATURES), BF16),
            vmem((D, FEATURES), BF16),
            vmem((D, FEATURES), BF16),
            vmem((FEATURES, D), BF16),
            vmem((4 * SEQ_RUN, RES, D), BF16),
            vmem((4, SEQ_RUN, RES, D), BF16),
            vmem((4, ROWS, FEATURES), BF16),
            vmem((4, ROWS, FEATURES), BF16),
            vmem((4, ROWS, FEATURES), BF16),
            vmem((8, 4, ROWS, 128), BF16),
            vmem((8, 4, ROWS, 128), BF16),
            vmem((8, 4, ROWS, 128), BF16),
            vmem((8, 4, ROWS, 128), BF16),
            vmem((32 * ROWS, 128), F32),
            vmem((128, SEQ_RUN * 128), BF16),
            vmem((128, SEQ_RUN * 128), BF16),
            vmem((128, SEQ_RUN * 128), BF16),
            vmem((128, SEQ_RUN * 128), BF16),
            vmem((8, 2, 16, 128), F32),
            vmem((8, 2, 16, 128), F32),
            vmem((2, 16, 128), F32),
            vmem((8, 2, 16, 128), F32),
            vmem((8, 2, 16, 128), BF16),
            vmem((16 * ROWS, 128), F32),
            vmem((8, 4, ROWS + ROWS // 2, 128), BF16),
            vmem((8, 4, ROWS + ROWS // 2, 128), BF16),
            vmem((4, SEQ_RUN, RES, D), BF16),
            dma((6,)), dma, dma((4,)), dma, dma((4,)),
            dma, dma, dma, dma, dma((2, 4)),
            dma, dma, dma, dma,
            dma, dma, dma, dma((4,)), dma((4,)),
            dma, dma((4,)), dma,
        ],
        compiler_params=pltpu.CompilerParams(
            collective_id=0, has_side_effects=True, vmem_limit_bytes=40 * 2**20
        ),
        cost_estimate=pl.CostEstimate(
            flops=2 * 10**9, bytes_accessed=5 * 10**6, transcendentals=2048
        ),
    )(activations, out_grad, w_query, w_key, w_value, w_output)


def solution(mesh):
    rows = P("seq", "res", None)
    return jax.shard_map(
        body,
        mesh=mesh,
        in_specs=(rows, rows, P(), P(), P(), P()),
        out_specs=rows,
        check_vma=False,
    )
```

time: 284 us -> 83.8 us (0.30)
  waiting for transfers between devices: 147 us -> 0 us
  blocking collectives: 80.5 us -> 0 us
  Pallas kernels: 0 us -> 76.2 us
  local copies, waits for them, and re-layouts: 28.5 us -> 7.27 us
  between operations: 13.8 us -> 0.02 us
  matrix products: 9.26 us -> 0 us
  other arithmetic: 4.85 us -> 0 us
    psum x1 -> x0, waiting for transfers between devices: 147 us -> none  [body(): parts = lax.psum(parts, ('seq', 'yh'))]
    all_to_all x2 -> x0, blocking collectives: 80.5 us -> none  [the longest x1 40.9 us: body(): lax.all_to_all(grads.reshape(32, chunk * res, 3 * HEAD_DIM), GROUP, split...]
    pallas_call x0 -> x1, Pallas kernels: none -> 76.2 us  [body(): pl.pallas_call(lambda *refs: kernel(scale, *refs), out_shape=jax.ShapeDty...]
    slice x9 -> x0, local copies, waits for them, and re-layouts: 11.5 us -> none  [the longest x5 8.29 us: body(): q, k, g, v = (packed[0], packed[1], packed[2], packed[3])]
    reshape x13 -> x0, local copies, waits for them, and re-layouts: 10.1 us -> none  [the longest x1 3.32 us: body(): packed = packed.reshape(32, chunk, res, 4, HEAD_DIM)]
    dot_general x12 -> x0, matrix products: 9.26 us -> none  [the longest x4 3.76 us: project(): jnp.dot(flat, weight, preferred_element_type=jnp.float32)]
    unnamed x18 -> x13, local copies, waits for them, and re-layouts: 0.36 us -> 7.27 us
    squeeze x6 -> x0, local copies, waits for them, and re-layouts: 3.03 us -> none  [the longest x3 2.07 us: body(): q, k, g, v = (packed[0], packed[1], packed[2], packed[3])]
  transfers between devices with their start and end apart: 1 -> 0, of which waited for: 1 -> 0; matrix products, arithmetic and copies ran while one was open for 0% -> 0% of each run, Pallas kernels for 0% -> 0%
where the time goes in v2:
time: 83.8 us; the launch traced here: 83.5 us
  Pallas kernels  76.2 us (91%)
  local copies, waits for them, and re-layouts  7.27 us (9%)
    pallas_call x1, Pallas kernels, body(): pl.pallas_call(lambda *refs: kernel(scale, *refs), out_shape=jax.ShapeDty...  76.2 us
    unnamed x13, local copies, waits for them, and re-layouts  7.27 us

profile of v2, /device:TPU:1, one launch (start us, length us, event | category | flops | bytes accessed | tf_op | source)
XLA Modules:
  0.0 83.5 jit_solution(18080970624857159127)
XLA Ops:
  0.0 0.0 copy-start
  0.0 1.1 %copy-done = bf16[768,512]{1,0:T(8,128)(2,1)S(1)} copy-done((bf16[768,512]{1,0:T(8,128)(2,1)S(1)}, bf16[768,512]{1,0:T(8,128)(2,1)}, u32[]{:S(2)}) %copy-start) | copy-done | bytes 786456
  1.1 0.0 copy-start.1
  1.1 1.1 %copy-done.1 = bf16[768,512]{1,0:T(8,128)(2,1)S(1)} copy-done((bf16[768,512]{1,0:T(8,128)(2,1)S(1)}, bf16[768,512]{1,0:T(8,128)(2,1)}, u32[]{:S(2)}) %copy-start.1) | copy-done | bytes 786456
  2.3 0.0 copy-start.2
  2.3 1.1 %copy-done.2 = bf16[768,512]{1,0:T(8,128)(2,1)S(1)} copy-done((bf16[768,512]{1,0:T(8,128)(2,1)S(1)}, bf16[768,512]{1,0:T(8,128)(2,1)}, u32[]{:S(2)}) %copy-start.2) | copy-done | bytes 786456
  3.4 0.0 copy-start.3
  3.4 1.1 %copy-done.3 = bf16[512,768]{1,0:T(8,128)(2,1)S(1)} copy-done((bf16[512,768]{1,0:T(8,128)(2,1)S(1)}, bf16[512,768]{1,0:T(8,128)(2,1)}, u32[]{:S(2)}) %copy-start.3) | copy-done | bytes 786456
  4.5 0.0 copy-start.4
  4.5 1.0 %copy-done.4 = bf16[64,4,768]{2,1,0:T(4,128)(2,1)S(1)} copy-done((bf16[64,4,768]{2,1,0:T(4,128)(2,1)S(1)}, bf16[64,4,768]{2,1,0:T(4,128)(2,1)}, u32[]{:S(2)}) %copy-start.4) | copy-done | bytes 393240
  5.5 0.0 copy-start.5
  5.5 1.0 %copy-done.5 = bf16[64,4,768]{2,1,0:T(4,128)(2,1)S(1)} copy-done((bf16[64,4,768]{2,1,0:T(4,128)(2,1)S(1)}, bf16[64,4,768]{2,1,0:T(4,128)(2,1)}, u32[]{:S(2)}) %copy-start.5) | copy-done | bytes 393240
  6.5 76.2 %shard_map.64 = bf16[64,4,768]{2,1,0:T(4,128)(2,1)S(1)} custom-call(bf16[64,4,768]{2,1,0:T(4,128)(2,1)S(1)} %copy-done.4, bf16[64,4,768]{2,1,0:T(4,128)(2,1)S(1)} %copy-done.5, bf16[768,512]{1,0:T(8,128)(2,1)S(1)} %copy-done, bf16[768,512]{1,0:T(8,128)(2,1)S(1)} %copy-done.1, bf16[768,512]{1,0:T(8,128)(2,1)S(1)} %copy-done.2, bf16[512,768]{1,0:T(8,128)(2,1)S(1)} %copy-done.3), custom_call_target="tpu_custom_call" | custom-call | flops 2000000000 | bytes 5000000 | tf_op jit(solution)/shard_map/pallas_call | solution.py:351
  82.7 0.7 copy.8
Async XLA Ops:
  0.0 1.1 %copy-start = (bf16[768,512]{1,0:T(8,128)(2,1)S(1)}, bf16[768,512]{1,0:T(8,128)(2,1)}, u32[]{:S(2)}) copy-start(bf16[768,512]{1,0:T(8,128)(2,1)} %refs_2_.1) | copy-start | bytes 2359300
  1.1 1.1 %copy-start.1 = (bf16[768,512]{1,0:T(8,128)(2,1)S(1)}, bf16[768,512]{1,0:T(8,128)(2,1)}, u32[]{:S(2)}) copy-start(bf16[768,512]{1,0:T(8,128)(2,1)} %refs_3_.1) | copy-start | bytes 2359300
  2.3 1.1 %copy-start.2 = (bf16[768,512]{1,0:T(8,128)(2,1)S(1)}, bf16[768,512]{1,0:T(8,128)(2,1)}, u32[]{:S(2)}) copy-start(bf16[768,512]{1,0:T(8,128)(2,1)} %refs_4_.1) | copy-start | bytes 2359300
  3.4 1.1 %copy-start.3 = (bf16[512,768]{1,0:T(8,128)(2,1)S(1)}, bf16[512,768]{1,0:T(8,128)(2,1)}, u32[]{:S(2)}) copy-start(bf16[512,768]{1,0:T(8,128)(2,1)} %refs_5_.1) | copy-start | bytes 2359300
  4.5 1.0 %copy-start.4 = (bf16[64,4,768]{2,1,0:T(4,128)(2,1)S(1)}, bf16[64,4,768]{2,1,0:T(4,128)(2,1)}, u32[]{:S(2)}) copy-start(bf16[64,4,768]{2,1,0:T(4,128)(2,1)} %refs_0_.1) | copy-start | bytes 1179652
  5.5 1.0 %copy-start.5 = (bf16[64,4,768]{2,1,0:T(4,128)(2,1)S(1)}, bf16[64,4,768]{2,1,0:T(4,128)(2,1)}, u32[]{:S(2)}) copy-start(bf16[64,4,768]{2,1,0:T(4,128)(2,1)} %refs_1_.1) | copy-start | bytes 1179652

commit v3 on v2

v3 whole, which is shorter than its diff:
```python
import math

import jax
import jax.numpy as jnp
from jax import lax
from jax.experimental import pallas as pl
from jax.experimental.pallas import tpu as pltpu
from jax.sharding import PartitionSpec as P

MESH = pl.DeviceIdType.MESH
F32, BF16 = jnp.float32, jnp.bfloat16
D = 768
FEATURES = 512
HEAD_DIM = 64
SEQ_RUN = 16
RES = 4
ROWS = SEQ_RUN * RES
HALF = ROWS // 2
NT = (((1,), (1,)), ((), ()))
TN = (((0,), (0,)), ((), ()))


def rows_dot(a, b, dims=(((1,), (0,)), ((), ()))):
    return lax.dot_general(a, b, dims, preferred_element_type=F32)


def kernel(
    scale,
    act, og, wq_hbm, wk_hbm, wv_hbm, wo_hbm,
    out,
    wq, wk, wv, wo, og_v, xr, g_near, g_own, g_recv, qkv_send, qkv_recv,
    wide, wide_g, q_all, k_all, v_all, g_all,
    part, part_recv, total, total_recv, probs, back_send, back_recv, out_send,
    load_sem, x_send_sem, x_recv_sem, near_send_sem, near_recv_sem, near_own_sem,
    g_send_sem, g_recv_sem, g_own_sem, qkv_send_sem, qkv_recv_sem, qkv_own_sem,
    part_send_sem, part_recv_sem, total_send_sem, total_recv_sem,
    probs_send_sem, probs_recv_sem, back_send_sem, back_recv_sem, back_own_sem,
    out_send_sem, out_recv_sem, out_own_sem,
):
    seq, res = lax.axis_index("seq"), lax.axis_index("res")
    ylo, z = seq // 8, seq % 8
    x, yh, core = res // 8, (res // 2) % 4, res % 2
    g = x * 2 + core
    w = yh * 2 + ylo

    def y_peer(h):
        return (seq, x * 8 + h * 2 + core)

    def head_peer(h):
        return (seq, (h // 2) * 8 + yh * 2 + h % 2)

    def z_peer(k):
        return (ylo * 8 + k, res)

    def line_peer(k):
        return ((k % 2) * 8 + z, x * 8 + (k // 2) * 2 + core)

    def run(h):
        return pl.ds(pl.multiple_of(h * SEQ_RUN, SEQ_RUN), SEQ_RUN)

    def wait_bytes(ref, sem):
        pltpu.make_async_copy(ref, ref, sem).wait()

    loads = [
        pltpu.make_async_copy(og, og_v, load_sem.at[0]),
        pltpu.make_async_copy(wo_hbm, wo, load_sem.at[1]),
        pltpu.make_async_copy(act.at[run(yh)], xr.at[yh], load_sem.at[2]),
        pltpu.make_async_copy(wq_hbm, wq, load_sem.at[3]),
        pltpu.make_async_copy(wk_hbm, wk, load_sem.at[4]),
        pltpu.make_async_copy(wv_hbm, wv, load_sem.at[5]),
    ]
    for load in loads:
        load.start()

    barrier = pltpu.get_barrier_semaphore()

    def greet(k, _):
        pl.semaphore_signal(barrier, inc=1, device_id=head_peer((g + k) % 8), device_id_type=MESH)
        pl.semaphore_signal(barrier, inc=1, device_id=z_peer((z + k) % 8), device_id_type=MESH)
        pl.semaphore_signal(barrier, inc=1, device_id=line_peer((w + k) % 8), device_id_type=MESH)
        return 0

    lax.fori_loop(1, 8, greet, 0)

    low = lax.broadcasted_iota(jnp.int32, (HALF, 128), 1) < HEAD_DIM

    def fold(top, bottom):
        turned = pltpu.roll(bottom, HEAD_DIM, 1)
        return jnp.where(low, top, turned), jnp.where(low, turned, top)

    loads[0].wait()
    loads[1].wait()
    grad_rows = rows_dot(og_v[...].reshape(4 * ROWS, D), wo[...], NT).astype(BF16)
    for c in range(4):
        for p in range(4):
            pair = grad_rows[c * ROWS : (c + 1) * ROWS, p * 128 : p * 128 + 128]
            g_near[2 * p, c], g_near[2 * p + 1, c] = fold(pair[:HALF], pair[HALF:])

    pl.semaphore_wait(barrier, 21)

    def x_copy(to, slot):
        return pltpu.make_async_remote_copy(
            act.at[run(to)], xr.at[slot], x_send_sem.at[to], x_recv_sem.at[slot],
            device_id=y_peer(to), device_id_type=MESH,
        )

    after, before, far = (yh + 1) % 4, (yh + 3) % 4, (yh + 2) % 4
    x_copy(after, yh).start()
    x_copy(before, yh).start()

    def send_near(k, _):
        to = (g + k) % 8
        pltpu.make_async_remote_copy(
            g_near.at[to], g_own.at[g], near_send_sem, near_recv_sem,
            device_id=head_peer(to), device_id_type=MESH,
        ).start()
        return 0

    lax.fori_loop(1, 8, send_near, 0)
    near_copy = pltpu.make_async_copy(g_near.at[g], g_own.at[g], near_own_sem)
    near_copy.start()

    def do_qkv(src):
        rows = xr[src].reshape(ROWS, D)
        for j, weight in enumerate((wq, wk, wv)):
            a = rows_dot(rows, weight[...]).astype(BF16)
            for p in range(4):
                pair = a[:, p * 128 : p * 128 + 128]
                even, odd = fold(pair[:HALF], pair[HALF:])
                qkv_send[2 * p, src, j * HALF : (j + 1) * HALF] = even
                qkv_send[2 * p + 1, src, j * HALF : (j + 1) * HALF] = odd

        def one(k, _):
            to = (g + k) % 8
            pltpu.make_async_remote_copy(
                qkv_send.at[to, src], qkv_recv.at[g, src], qkv_send_sem, qkv_recv_sem,
                device_id=head_peer(to), device_id_type=MESH,
            ).start()
            return 0

        lax.fori_loop(1, 8, one, 0)
        pltpu.make_async_copy(qkv_send.at[g, src], qkv_recv.at[g, src], qkv_own_sem.at[src]).start()

    for load in loads[2:]:
        load.wait()
    do_qkv(yh)

    x_copy(after, yh).wait_send()
    x_copy(before, yh).wait_send()
    x_copy(far, yh).start()

    def near_qkv(k, _):
        src = (yh + 1 + 2 * k) % 4
        x_copy(src, src).wait_recv()
        do_qkv(src)
        return 0

    lax.fori_loop(0, 2, near_qkv, 0)

    def g_copy(to, slot):
        return pltpu.make_async_remote_copy(
            g_own.at[:, to], g_recv.at[:, slot], g_send_sem, g_recv_sem,
            device_id=y_peer(to), device_id_type=MESH,
        )

    wait_bytes(g_own.at[pl.ds(0, 7)], near_recv_sem)
    near_copy.wait()
    x_copy(far, yh).wait_send()
    g_copy(after, yh).start()
    g_copy(before, yh).start()
    g_copy(far, yh).start()
    own_g = pltpu.make_async_copy(g_own.at[:, yh], g_recv.at[:, yh], g_own_sem)
    own_g.start()

    x_copy(far, far).wait_recv()
    do_qkv(far)

    wait_bytes(qkv_recv.at[pl.ds(0, 7)], qkv_recv_sem)
    for src in range(4):
        pltpu.make_async_copy(qkv_send.at[g, src], qkv_recv.at[g, src], qkv_own_sem.at[src]).wait()
    wide[...] = qkv_recv[...].reshape(32 * 3 * HALF, 128).astype(F32)

    def gather(source, first, stride):
        return jnp.concatenate(
            [source[pl.ds(first + r, 32, stride=stride), :] for r in range(RES)], axis=0
        ).astype(BF16)

    for s in range(SEQ_RUN // 2):
        lanes = slice(s * 128, s * 128 + 128)
        for j, keep in enumerate((q_all, k_all, v_all)):
            keep[:, lanes] = gather(wide, j * HALF + s * RES, 3 * HALF)
    part[:, 0] = rows_dot(q_all[...], k_all[...], NT).reshape(8, 16, 128)

    wait_bytes(g_recv.at[:, pl.ds(0, 3)], g_recv_sem)
    own_g.wait()
    wide_g[...] = g_recv[...].reshape(32 * HALF, 128).astype(F32)
    for s in range(SEQ_RUN // 2):
        g_all[:, s * 128 : s * 128 + 128] = gather(wide_g, s * RES, HALF)
    part[:, 1] = rows_dot(g_all[...], v_all[...], NT).reshape(8, 16, 128)

    def send_part(k, _):
        to = (z + k) % 8
        pltpu.make_async_remote_copy(
            part.at[to], part_recv.at[z], part_send_sem, part_recv_sem,
            device_id=z_peer(to), device_id_type=MESH,
        ).start()
        return 0

    lax.fori_loop(1, 8, send_part, 0)
    part_recv[z] = part[z]
    wait_bytes(part_recv.at[pl.ds(0, 7)], part_recv_sem)
    total[...] = jnp.sum(part_recv[...], axis=0)

    def send_total(k, _):
        to = (w + k) % 8
        pltpu.make_async_remote_copy(
            total, total_recv.at[w], total_send_sem, total_recv_sem,
            device_id=line_peer(to), device_id_type=MESH,
        ).start()
        return 0

    lax.fori_loop(1, 8, send_total, 0)
    total_recv[w] = total[...]
    wait_bytes(total_recv.at[pl.ds(0, 7)], total_recv_sem)
    sums = jnp.sum(total_recv[...], axis=0)
    scores, prob_grad = scale * sums[0], sums[1]
    grown = jnp.exp(scores - jnp.max(scores, axis=-1, keepdims=True))
    probability = grown / jnp.sum(grown, axis=-1, keepdims=True)
    row_total = jnp.sum(probability * prob_grad, axis=-1, keepdims=True)
    probs[z, 0] = (scale * probability * (prob_grad - row_total)).astype(BF16)
    probs[z, 1] = probability.astype(BF16)

    def send_probs(k, _):
        to = (z + k) % 8
        pltpu.make_async_remote_copy(
            probs.at[z], probs.at[z], probs_send_sem, probs_recv_sem,
            device_id=z_peer(to), device_id_type=MESH,
        ).start()
        return 0

    lax.fori_loop(1, 8, send_probs, 0)
    wait_bytes(probs.at[pl.ds(0, 7)], probs_recv_sem)
    score_grad = probs[:, 0].reshape(128, 128)
    prob_low = probs[:, 1].reshape(128, 128)

    for j, grad in enumerate(
        (
            rows_dot(score_grad, k_all[...]),
            rows_dot(score_grad, q_all[...], TN),
            rows_dot(prob_low, g_all[...], TN),
        )
    ):
        for s in range(SEQ_RUN // 2):
            for r in range(RES):
                wide[pl.ds(j * HALF + s * RES + r, 32, stride=3 * HALF), :] = grad[
                    r * 32 : r * 32 + 32, s * 128 : s * 128 + 128
                ]
    back_send[...] = wide[...].astype(BF16).reshape(8, 4, 3 * HALF, 128)

    def place(k):
        back = 3 - k
        return (yh + back + back // 2 - 2 * (back // 3)) % 4

    def send_back(k, _):
        src = place(k)

        def one(j, _):
            to = (g + j) % 8
            pltpu.make_async_remote_copy(
                back_send.at[to, src], back_recv.at[g, src], back_send_sem, back_recv_sem.at[src],
                device_id=head_peer(to), device_id_type=MESH,
            ).start()
            return 0

        lax.fori_loop(1, 8, one, 0)
        pltpu.make_async_copy(back_send.at[g, src], back_recv.at[g, src], back_own_sem.at[src]).start()
        return 0

    lax.fori_loop(0, 4, send_back, 0)

    low_back = lax.broadcasted_iota(jnp.int32, (3 * HALF, 128), 1) < HEAD_DIM

    def out_copy(to, slot):
        return pltpu.make_async_remote_copy(
            out_send.at[to], out.at[run(slot)], out_send_sem, out_recv_sem.at[slot],
            device_id=y_peer(to), device_id_type=MESH,
        )

    def finish(src):
        wait_bytes(back_recv.at[pl.ds(0, 7), src], back_recv_sem.at[src])
        pltpu.make_async_copy(back_send.at[g, src], back_recv.at[g, src], back_own_sem.at[src]).wait()
        tops, bottoms = [], []
        for p in range(4):
            a, b = back_recv[2 * p, src], back_recv[2 * p + 1, src]
            tops.append(jnp.where(low_back, a, b))
            bottoms.append(pltpu.roll(jnp.where(low_back, b, a), HEAD_DIM, 1))
        top, bottom = jnp.concatenate(tops, axis=1), jnp.concatenate(bottoms, axis=1)
        grad = None
        for j, weight in enumerate((wq, wk, wv)):
            rows = slice(j * HALF, (j + 1) * HALF)
            term = rows_dot(jnp.concatenate([top[rows], bottom[rows]], axis=0), weight[...], NT)
            grad = term if grad is None else grad + term
        out_send[src] = grad.astype(BF16).reshape(SEQ_RUN, RES, D)

    def finish_far(k, _):
        src = place(k)
        finish(src)
        out_copy(src, yh).start()
        return 0

    lax.fori_loop(0, 3, finish_far, 0)
    finish(yh)
    own_out = pltpu.make_async_copy(out_send.at[yh], out.at[run(yh)], out_own_sem)
    own_out.start()

    wait_bytes(g_own.at[pl.ds(0, 7)], near_send_sem)
    wait_bytes(g_own.at[:, pl.ds(0, 3)], g_send_sem)
    wait_bytes(qkv_send.at[pl.ds(0, 7)], qkv_send_sem)
    wait_bytes(part_recv.at[pl.ds(0, 7)], part_send_sem)
    wait_bytes(total_recv.at[pl.ds(0, 7)], total_send_sem)
    wait_bytes(probs.at[pl.ds(0, 7)], probs_send_sem)
    wait_bytes(back_send.at[pl.ds(0, 7)], back_send_sem)
    wait_bytes(out_send.at[pl.ds(0, 3)], out_send_sem)

    def wait_out(k, _):
        src = (yh + k) % 4
        out_copy(src, src).wait_recv()
        return 0

    lax.fori_loop(1, 4, wait_out, 0)
    own_out.wait()


def body(activations, out_grad, w_query, w_key, w_value, w_output):
    seqs_total = activations.shape[0] * lax.axis_size("seq")
    scale = 1.0 / math.sqrt(HEAD_DIM * seqs_total)
    hbm = pl.BlockSpec(memory_space=pltpu.HBM)
    dma = pltpu.SemaphoreType.DMA
    vmem = pltpu.VMEM
    return pl.pallas_call(
        lambda *refs: kernel(scale, *refs),
        out_shape=jax.ShapeDtypeStruct(activations.shape, BF16),
        in_specs=[hbm] * 6,
        out_specs=pl.BlockSpec(memory_space=pl.ANY),
        scratch_shapes=[
            vmem((D, FEATURES), BF16),
            vmem((D, FEATURES), BF16),
            vmem((D, FEATURES), BF16),
            vmem((FEATURES, D), BF16),
            vmem((4 * SEQ_RUN, RES, D), BF16),
            vmem((4, SEQ_RUN, RES, D), BF16),
            vmem((8, 4, HALF, 128), BF16),
            vmem((8, 4, HALF, 128), BF16),
            vmem((8, 4, HALF, 128), BF16),
            vmem((8, 4, 3 * HALF, 128), BF16),
            vmem((8, 4, 3 * HALF, 128), BF16),
            vmem((32 * 3 * HALF, 128), F32),
            vmem((32 * HALF, 128), F32),
            vmem((128, SEQ_RUN * HEAD_DIM), BF16),
            vmem((128, SEQ_RUN * HEAD_DIM), BF16),
            vmem((128, SEQ_RUN * HEAD_DIM), BF16),
            vmem((128, SEQ_RUN * HEAD_DIM), BF16),
            vmem((8, 2, 16, 128), F32),
            vmem((8, 2, 16, 128), F32),
            vmem((2, 16, 128), F32),
            vmem((8, 2, 16, 128), F32),
            vmem((8, 2, 16, 128), BF16),
            vmem((8, 4, 3 * HALF, 128), BF16),
            vmem((8, 4, 3 * HALF, 128), BF16),
            vmem((4, SEQ_RUN, RES, D), BF16),
            dma((6,)), dma((4,)), dma((4,)), dma, dma, dma,
            dma, dma, dma, dma, dma, dma((4,)),
            dma, dma, dma, dma,
            dma, dma, dma, dma((4,)), dma((4,)),
            dma, dma((4,)), dma,
        ],
        compiler_params=pltpu.CompilerParams(
            collective_id=0, has_side_effects=True, vmem_limit_bytes=54 * 2**20
        ),
        cost_estimate=pl.CostEstimate(
            flops=2 * 10**9, bytes_accessed=5 * 10**6, transcendentals=2048
        ),
    )(activations, out_grad, w_query, w_key, w_value, w_output)


def solution(mesh):
    rows = P("seq", "res", None)
    return jax.shard_map(
        body,
        mesh=mesh,
        in_specs=(rows, rows, P(), P(), P(), P()),
        out_specs=rows,
        check_vma=False,
    )
```

time: 83.8 us -> 72.7 us (0.87)
  Pallas kernels: 76.2 us -> 70.6 us
  local copies, waits for them, and re-layouts: 7.27 us -> 1.88 us
    pallas_call x1, Pallas kernels: 76.2 us -> 70.6 us  [body(): pl.pallas_call(lambda *refs: kernel(scale, *refs), out_shape=jax.ShapeDty...]
    unnamed x13 -> x1, local copies, waits for them, and re-layouts: 7.27 us -> 1.88 us
where the time goes in v3:
time: 72.7 us; the launch traced here: 72.5 us
  Pallas kernels  70.6 us (97%)
  local copies, waits for them, and re-layouts  1.88 us (3%)
    pallas_call x1, Pallas kernels, body(): pl.pallas_call(lambda *refs: kernel(scale, *refs), out_shape=jax.ShapeDty...  70.6 us
    unnamed x1, local copies, waits for them, and re-layouts  1.88 us

profile of v3, /device:TPU:1, one launch (start us, length us, event | category | flops | bytes accessed | tf_op | source)
XLA Modules:
  0.0 72.5 jit_solution(16525233937997926810)
XLA Ops:
  0.0 70.6 %shard_map.64 = bf16[64,4,768]{2,1,0:T(4,128)(2,1)} custom-call(bf16[64,4,768]{2,1,0:T(4,128)(2,1)} %refs_0_.1, bf16[64,4,768]{2,1,0:T(4,128)(2,1)} %refs_1_.1, bf16[768,512]{1,0:T(8,128)(2,1)} %refs_2_.1, bf16[768,512]{1,0:T(8,128)(2,1)} %refs_3_.1, bf16[768,512]{1,0:T(8,128)(2,1)} %refs_4_.1, bf16[512,768]{1,0:T(8,128)(2,1)} %refs_5_.1), custom_call_target="tpu_custom_call" | custom-call | flops 2000000000 | bytes 5000000 | tf_op jit(solution)/shard_map/pallas_call | solution.py:340
  70.6 1.9 %copy.8 = bf16[64,4,768]{2,1,0:T(4,128)(2,1)} copy(bf16[64,4,768]{2,1,0:T(4,128)(2,1)} %shard_map.64) | data formatting | bytes 786432

commit v4 on v3

--- a/solution.py
+++ b/solution.py
@@ -29,7 +29,7 @@
     act, og, wq_hbm, wk_hbm, wv_hbm, wo_hbm,
     out,
     wq, wk, wv, wo, og_v, xr, g_near, g_own, g_recv, qkv_send, qkv_recv,
-    wide, wide_g, q_all, k_all, v_all, g_all,
+    wide, wide_g, q_all, k_all, v_all, g_all, grads,
     part, part_recv, total, total_recv, probs, back_send, back_recv, out_send,
     load_sem, x_send_sem, x_recv_sem, near_send_sem, near_recv_sem, near_own_sem,
     g_send_sem, g_recv_sem, g_own_sem, qkv_send_sem, qkv_recv_sem, qkv_own_sem,
@@ -82,6 +82,18 @@
 
     lax.fori_loop(1, 8, greet, 0)
 
+    pl.semaphore_wait(barrier, 21)
+
+    def x_copy(to, slot):
+        return pltpu.make_async_remote_copy(
+            act.at[run(to)], xr.at[slot], x_send_sem.at[to], x_recv_sem.at[slot],
+            device_id=y_peer(to), device_id_type=MESH,
+        )
+
+    after, before, far = (yh + 1) % 4, (yh + 3) % 4, (yh + 2) % 4
+    x_copy(after, yh).start()
+    x_copy(before, yh).start()
+
     low = lax.broadcasted_iota(jnp.int32, (HALF, 128), 1) < HEAD_DIM
 
     def fold(top, bottom):
@@ -96,17 +108,8 @@
             pair = grad_rows[c * ROWS : (c + 1) * ROWS, p * 128 : p * 128 + 128]
             g_near[2 * p, c], g_near[2 * p + 1, c] = fold(pair[:HALF], pair[HALF:])
 
-    pl.semaphore_wait(barrier, 21)
-
-    def x_copy(to, slot):
-        return pltpu.make_async_remote_copy(
-            act.at[run(to)], xr.at[slot], x_send_sem.at[to], x_recv_sem.at[slot],
-            device_id=y_peer(to), device_id_type=MESH,
-        )
-
-    after, before, far = (yh + 1) % 4, (yh + 3) % 4, (yh + 2) % 4
-    x_copy(after, yh).start()
-    x_copy(before, yh).start()
+    def near_first(k):
+        return k + k // 2 - 2 * (k // 3)
 
     def send_near(k, _):
         to = (g + k) % 8
@@ -119,6 +122,7 @@
     lax.fori_loop(1, 8, send_near, 0)
     near_copy = pltpu.make_async_copy(g_near.at[g], g_own.at[g], near_own_sem)
     near_copy.start()
+    x_copy(far, yh).start()
 
     def do_qkv(src):
         rows = xr[src].reshape(ROWS, D)
@@ -127,75 +131,91 @@
             for p in range(4):
                 pair = a[:, p * 128 : p * 128 + 128]
                 even, odd = fold(pair[:HALF], pair[HALF:])
-                qkv_send[2 * p, src, j * HALF : (j + 1) * HALF] = even
-                qkv_send[2 * p + 1, src, j * HALF : (j + 1) * HALF] = odd
+                qkv_send[src, 2 * p, j * HALF : (j + 1) * HALF] = even
+                qkv_send[src, 2 * p + 1, j * HALF : (j + 1) * HALF] = odd
 
         def one(k, _):
             to = (g + k) % 8
             pltpu.make_async_remote_copy(
-                qkv_send.at[to, src], qkv_recv.at[g, src], qkv_send_sem, qkv_recv_sem,
+                qkv_send.at[src, to], qkv_recv.at[src, g], qkv_send_sem, qkv_recv_sem.at[src],
                 device_id=head_peer(to), device_id_type=MESH,
             ).start()
             return 0
 
         lax.fori_loop(1, 8, one, 0)
-        pltpu.make_async_copy(qkv_send.at[g, src], qkv_recv.at[g, src], qkv_own_sem.at[src]).start()
+        pltpu.make_async_copy(qkv_send.at[src, g], qkv_recv.at[src, g], qkv_own_sem.at[src]).start()
 
     for load in loads[2:]:
         load.wait()
     do_qkv(yh)
 
-    x_copy(after, yh).wait_send()
-    x_copy(before, yh).wait_send()
-    x_copy(far, yh).start()
+    def g_copy(to, slot):
+        return pltpu.make_async_remote_copy(
+            g_own.at[:, to], g_recv.at[slot], g_send_sem, g_recv_sem.at[slot],
+            device_id=y_peer(to), device_id_type=MESH,
+        )
 
     def near_qkv(k, _):
         src = (yh + 1 + 2 * k) % 4
         x_copy(src, src).wait_recv()
         do_qkv(src)
+
+        @pl.when(k == 0)
+        def _():
+            wait_bytes(g_own.at[pl.ds(0, 7)], near_recv_sem)
+            near_copy.wait()
+            g_copy(after, yh).start()
+            g_copy(before, yh).start()
+            g_copy(far, yh).start()
+
         return 0
 
     lax.fori_loop(0, 2, near_qkv, 0)
-
-    def g_copy(to, slot):
-        return pltpu.make_async_remote_copy(
-            g_own.at[:, to], g_recv.at[:, slot], g_send_sem, g_recv_sem,
-            device_id=y_peer(to), device_id_type=MESH,
-        )
-
-    wait_bytes(g_own.at[pl.ds(0, 7)], near_recv_sem)
-    near_copy.wait()
-    x_copy(far, yh).wait_send()
-    g_copy(after, yh).start()
-    g_copy(before, yh).start()
-    g_copy(far, yh).start()
-    own_g = pltpu.make_async_copy(g_own.at[:, yh], g_recv.at[:, yh], g_own_sem)
+    own_g = pltpu.make_async_copy(g_own.at[:, yh], g_recv.at[yh], g_own_sem)
     own_g.start()
+
+    def gather(source, first, stride):
+        return jnp.concatenate(
+            [source[pl.ds(first + r, 8, stride=stride), :] for r in range(RES)], axis=0
+        ).astype(BF16)
+
+    def chunk(src):
+        return pl.ds(pl.multiple_of(src * 32, 32), 32)
+
+    def take_qkv(src):
+        wait_bytes(qkv_recv.at[src, pl.ds(0, 7)], qkv_recv_sem.at[src])
+        pltpu.make_async_copy(qkv_send.at[src, g], qkv_recv.at[src, g], qkv_own_sem.at[src]).wait()
+        wide[...] = qkv_recv[src].reshape(8 * 3 * HALF, 128).astype(F32)
+        for s in range(SEQ_RUN // 2):
+            for j, keep in enumerate((q_all, k_all, v_all)):
+                keep[chunk(src), s * 128 : s * 128 + 128] = gather(wide, j * HALF + s * RES, 3 * HALF)
+
+    def take_g(src):
+        wide_g[...] = g_recv[src].reshape(8 * HALF, 128).astype(F32)
+        for s in range(SEQ_RUN // 2):
+            g_all[chunk(src), s * 128 : s * 128 + 128] = gather(wide_g, s * RES, HALF)
+
+    take_qkv(yh)
+    own_g.wait()
+    take_g(yh)
 
     x_copy(far, far).wait_recv()
     do_qkv(far)
 
-    wait_bytes(qkv_recv.at[pl.ds(0, 7)], qkv_recv_sem)
-    for src in range(4):
-        pltpu.make_async_copy(qkv_send.at[g, src], qkv_recv.at[g, src], qkv_own_sem.at[src]).wait()
-    wide[...] = qkv_recv[...].reshape(32 * 3 * HALF, 128).astype(F32)
-
-    def gather(source, first, stride):
-        return jnp.concatenate(
-            [source[pl.ds(first + r, 32, stride=stride), :] for r in range(RES)], axis=0
-        ).astype(BF16)
-
-    for s in range(SEQ_RUN // 2):
-        lanes = slice(s * 128, s * 128 + 128)
-        for j, keep in enumerate((q_all, k_all, v_all)):
-            keep[:, lanes] = gather(wide, j * HALF + s * RES, 3 * HALF)
+    def next_qkv(k, _):
+        take_qkv((yh + near_first(k)) % 4)
+        return 0
+
+    lax.fori_loop(1, 4, next_qkv, 0)
     part[:, 0] = rows_dot(q_all[...], k_all[...], NT).reshape(8, 16, 128)
 
-    wait_bytes(g_recv.at[:, pl.ds(0, 3)], g_recv_sem)
-    own_g.wait()
-    wide_g[...] = g_recv[...].reshape(32 * HALF, 128).astype(F32)
-    for s in range(SEQ_RUN // 2):
-        g_all[:, s * 128 : s * 128 + 128] = gather(wide_g, s * RES, HALF)
+    def next_g(k, _):
+        src = (yh + near_first(k)) % 4
+        g_copy(src, src).wait_recv()
+        take_g(src)
+        return 0
+
+    lax.fori_loop(1, 4, next_g, 0)
     part[:, 1] = rows_dot(g_all[...], v_all[...], NT).reshape(8, 16, 128)
 
     def send_part(k, _):
@@ -243,92 +263,103 @@
     score_grad = probs[:, 0].reshape(128, 128)
     prob_low = probs[:, 1].reshape(128, 128)
 
-    for j, grad in enumerate(
-        (
-            rows_dot(score_grad, k_all[...]),
-            rows_dot(score_grad, q_all[...], TN),
-            rows_dot(prob_low, g_all[...], TN),
-        )
-    ):
-        for s in range(SEQ_RUN // 2):
-            for r in range(RES):
-                wide[pl.ds(j * HALF + s * RES + r, 32, stride=3 * HALF), :] = grad[
-                    r * 32 : r * 32 + 32, s * 128 : s * 128 + 128
-                ]
-    back_send[...] = wide[...].astype(BF16).reshape(8, 4, 3 * HALF, 128)
+    grads[0] = rows_dot(score_grad, k_all[...])
+    grads[1] = rows_dot(score_grad, q_all[...], TN)
+    grads[2] = rows_dot(prob_low, g_all[...], TN)
 
     def place(k):
-        back = 3 - k
-        return (yh + back + back // 2 - 2 * (back // 3)) % 4
+        return (yh + near_first(3 - k)) % 4
 
     def send_back(k, _):
         src = place(k)
+        for j in range(3):
+            for s in range(SEQ_RUN // 2):
+                for r in range(RES):
+                    rows = pl.ds(pl.multiple_of(src * 32 + r * 8, 8), 8)
+                    wide[pl.ds(j * HALF + s * RES + r, 8, stride=3 * HALF), :] = grads[
+                        j, rows, s * 128 : s * 128 + 128
+                    ]
+        back_send[src] = wide[...].astype(BF16).reshape(8, 3 * HALF, 128)
 
         def one(j, _):
             to = (g + j) % 8
             pltpu.make_async_remote_copy(
-                back_send.at[to, src], back_recv.at[g, src], back_send_sem, back_recv_sem.at[src],
+                back_send.at[src, to], back_recv.at[src, g], back_send_sem, back_recv_sem.at[src],
                 device_id=head_peer(to), device_id_type=MESH,
             ).start()
             return 0
 
         lax.fori_loop(1, 8, one, 0)
-        pltpu.make_async_copy(back_send.at[g, src], back_recv.at[g, src], back_own_sem.at[src]).start()
+        pltpu.make_async_copy(back_send.at[src, g], back_recv.at[src, g], back_own_sem.at[src]).start()
         return 0
 
     lax.fori_loop(0, 4, send_back, 0)
 
     low_back = lax.broadcasted_iota(jnp.int32, (3 * HALF, 128), 1) < HEAD_DIM
 
-    def out_copy(to, slot):
+    def out_copy(to, slot, n):
         return pltpu.make_async_remote_copy(
-            out_send.at[to], out.at[run(slot)], out_send_sem, out_recv_sem.at[slot],
+            out_send.at[to, n], out.at[run(slot), :, pl.ds(n * (D // 2), D // 2)], out_send_sem, out_recv_sem.at[slot, n],
             device_id=y_peer(to), device_id_type=MESH,
         )
 
-    def finish(src):
-        wait_bytes(back_recv.at[pl.ds(0, 7), src], back_recv_sem.at[src])
-        pltpu.make_async_copy(back_send.at[g, src], back_recv.at[g, src], back_own_sem.at[src]).wait()
+    def finish(src, remote):
+        wait_bytes(back_recv.at[src, pl.ds(0, 7)], back_recv_sem.at[src])
+        pltpu.make_async_copy(back_send.at[src, g], back_recv.at[src, g], back_own_sem.at[src]).wait()
         tops, bottoms = [], []
         for p in range(4):
-            a, b = back_recv[2 * p, src], back_recv[2 * p + 1, src]
+            a, b = back_recv[src, 2 * p], back_recv[src, 2 * p + 1]
             tops.append(jnp.where(low_back, a, b))
             bottoms.append(pltpu.roll(jnp.where(low_back, b, a), HEAD_DIM, 1))
         top, bottom = jnp.concatenate(tops, axis=1), jnp.concatenate(bottoms, axis=1)
-        grad = None
-        for j, weight in enumerate((wq, wk, wv)):
-            rows = slice(j * HALF, (j + 1) * HALF)
-            term = rows_dot(jnp.concatenate([top[rows], bottom[rows]], axis=0), weight[...], NT)
-            grad = term if grad is None else grad + term
-        out_send[src] = grad.astype(BF16).reshape(SEQ_RUN, RES, D)
+        sides = [
+            jnp.concatenate([top[j * HALF : (j + 1) * HALF], bottom[j * HALF : (j + 1) * HALF]], axis=0)
+            for j in range(3)
+        ]
+        for n in range(2):
+            cols = slice(n * (D // 2), (n + 1) * (D // 2))
+            grad = None
+            for side, weight in zip(sides, (wq, wk, wv)):
+                term = rows_dot(side, weight[cols, :], NT)
+                grad = term if grad is None else grad + term
+            out_send[src, n] = grad.astype(BF16).reshape(SEQ_RUN, RES, D // 2)
+            if remote:
+                out_copy(src, yh, n).start()
 
     def finish_far(k, _):
         src = place(k)
-        finish(src)
-        out_copy(src, yh).start()
+        finish(src, True)
         return 0
 
     lax.fori_loop(0, 3, finish_far, 0)
-    finish(yh)
-    own_out = pltpu.make_async_copy(out_send.at[yh], out.at[run(yh)], out_own_sem)
-    own_out.start()
+    finish(yh, False)
+    own_outs = [
+        pltpu.make_async_copy(out_send.at[yh, n], out.at[run(yh), :, pl.ds(n * (D // 2), D // 2)], out_own_sem.at[n])
+        for n in range(2)
+    ]
+    for own_out in own_outs:
+        own_out.start()
 
     wait_bytes(g_own.at[pl.ds(0, 7)], near_send_sem)
-    wait_bytes(g_own.at[:, pl.ds(0, 3)], g_send_sem)
-    wait_bytes(qkv_send.at[pl.ds(0, 7)], qkv_send_sem)
+    for to in (after, before, far):
+        x_copy(to, yh).wait_send()
+    wait_bytes(g_recv.at[pl.ds(0, 3)], g_send_sem)
+    wait_bytes(qkv_send.at[:, pl.ds(0, 7)], qkv_send_sem)
     wait_bytes(part_recv.at[pl.ds(0, 7)], part_send_sem)
     wait_bytes(total_recv.at[pl.ds(0, 7)], total_send_sem)
     wait_bytes(probs.at[pl.ds(0, 7)], probs_send_sem)
-    wait_bytes(back_send.at[pl.ds(0, 7)], back_send_sem)
+    wait_bytes(back_send.at[:, pl.ds(0, 7)], back_send_sem)
     wait_bytes(out_send.at[pl.ds(0, 3)], out_send_sem)
 
     def wait_out(k, _):
         src = (yh + k) % 4
-        out_copy(src, src).wait_recv()
+        for n in range(2):
+            out_copy(src, src, n).wait_recv()
         return 0
 
     lax.fori_loop(1, 4, wait_out, 0)
-    own_out.wait()
+    for own_out in own_outs:
+        own_out.wait()
 
 
 def body(activations, out_grad, w_query, w_key, w_value, w_output):
@@ -351,31 +382,32 @@
             vmem((4, SEQ_RUN, RES, D), BF16),
             vmem((8, 4, HALF, 128), BF16),
             vmem((8, 4, HALF, 128), BF16),
-            vmem((8, 4, HALF, 128), BF16),
-            vmem((8, 4, 3 * HALF, 128), BF16),
-            vmem((8, 4, 3 * HALF, 128), BF16),
-            vmem((32 * 3 * HALF, 128), F32),
-            vmem((32 * HALF, 128), F32),
+            vmem((4, 8, HALF, 128), BF16),
+            vmem((4, 8, 3 * HALF, 128), BF16),
+            vmem((4, 8, 3 * HALF, 128), BF16),
+            vmem((8 * 3 * HALF, 128), F32),
+            vmem((8 * HALF, 128), F32),
             vmem((128, SEQ_RUN * HEAD_DIM), BF16),
             vmem((128, SEQ_RUN * HEAD_DIM), BF16),
             vmem((128, SEQ_RUN * HEAD_DIM), BF16),
             vmem((128, SEQ_RUN * HEAD_DIM), BF16),
+            vmem((3, 128, SEQ_RUN * HEAD_DIM), F32),
             vmem((8, 2, 16, 128), F32),
             vmem((8, 2, 16, 128), F32),
             vmem((2, 16, 128), F32),
             vmem((8, 2, 16, 128), F32),
             vmem((8, 2, 16, 128), BF16),
-            vmem((8, 4, 3 * HALF, 128), BF16),
-            vmem((8, 4, 3 * HALF, 128), BF16),
-            vmem((4, SEQ_RUN, RES, D), BF16),
+            vmem((4, 8, 3 * HALF, 128), BF16),
+            vmem((4, 8, 3 * HALF, 128), BF16),
+            vmem((4, 2, SEQ_RUN, RES, D // 2), BF16),
             dma((6,)), dma((4,)), dma((4,)), dma, dma, dma,
-            dma, dma, dma, dma, dma, dma((4,)),
+            dma, dma((4,)), dma, dma, dma((4,)), dma((4,)),
             dma, dma, dma, dma,
             dma, dma, dma, dma((4,)), dma((4,)),
-            dma, dma((4,)), dma,
+            dma, dma((4, 2)), dma((2,)),
         ],
         compiler_params=pltpu.CompilerParams(
-            collective_id=0, has_side_effects=True, vmem_limit_bytes=54 * 2**20
+            collective_id=0, has_side_effects=True, vmem_limit_bytes=54784 * 2**10
         ),
         cost_estimate=pl.CostEstimate(
             flops=2 * 10**9, bytes_accessed=5 * 10**6, transcendentals=2048

time: 72.7 us -> 70.2 us (0.966)
  Pallas kernels: 70.6 us -> 69.4 us
  local copies, waits for them, and re-layouts: 1.88 us -> 0.75 us
    pallas_call x1, Pallas kernels: 70.6 us -> 69.4 us  [body(): pl.pallas_call(lambda *refs: kernel(scale, *refs), out_shape=jax.ShapeDty...]
    unnamed x1, local copies, waits for them, and re-layouts: 1.88 us -> 0.75 us
where the time goes in v4:
time: 70.2 us; the launch traced here: 70.1 us
  Pallas kernels  69.4 us (99%)
  local copies, waits for them, and re-layouts  0.75 us (1%)
    pallas_call x1, Pallas kernels, body(): pl.pallas_call(lambda *refs: kernel(scale, *refs), out_shape=jax.ShapeDty...  69.4 us

profile of v4, /device:TPU:1, one launch (start us, length us, event | category | flops | bytes accessed | tf_op | source)
XLA Modules:
  0.0 70.1 jit_solution(11942272684263751329)
XLA Ops:
  0.0 69.4 %shard_map.64 = bf16[64,4,768]{2,1,0:T(4,128)(2,1)S(1)} custom-call(bf16[64,4,768]{2,1,0:T(4,128)(2,1)} %refs_0_.1, bf16[64,4,768]{2,1,0:T(4,128)(2,1)} %refs_1_.1, bf16[768,512]{1,0:T(8,128)(2,1)} %refs_2_.1, bf16[768,512]{1,0:T(8,128)(2,1)} %refs_3_.1, bf16[768,512]{1,0:T(8,128)(2,1)} %refs_4_.1, bf16[512,768]{1,0:T(8,128)(2,1)} %refs_5_.1), custom_call_target="tpu_custom_call" | custom-call | flops 2000000000 | bytes 5000000 | tf_op jit(solution)/shard_map/pallas_call | solution.py:371
  69.4 0.7 %copy.8 = bf16[64,4,768]{2,1,0:T(4,128)(2,1)} copy(bf16[64,4,768]{2,1,0:T(4,128)(2,1)S(1)} %shard_map.64) | data formatting | bytes 786432

commit v5 on v4

--- a/solution.py
+++ b/solution.py
@@ -16,6 +16,8 @@
 RES = 4
 ROWS = SEQ_RUN * RES
 HALF = ROWS // 2
+QUARTER = SEQ_RUN // 4
+PART = HALF // 2
 NT = (((1,), (1,)), ((), ()))
 TN = (((0,), (0,)), ((), ()))
 
@@ -30,11 +32,12 @@
     out,
     wq, wk, wv, wo, og_v, xr, g_near, g_own, g_recv, qkv_send, qkv_recv,
     wide, wide_g, q_all, k_all, v_all, g_all, grads,
-    part, part_recv, total, total_recv, probs, back_send, back_recv, out_send,
+    part, part_recv, total, total_recv, probs, wide_back, back_send, back_recv, early, late, out_send,
     load_sem, x_send_sem, x_recv_sem, near_send_sem, near_recv_sem, near_own_sem,
     g_send_sem, g_recv_sem, g_own_sem, qkv_send_sem, qkv_recv_sem, qkv_own_sem,
     part_send_sem, part_recv_sem, total_send_sem, total_recv_sem,
     probs_send_sem, probs_recv_sem, back_send_sem, back_recv_sem, back_own_sem,
+    early_send_sem, early_recv_sem, late_send_sem, late_recv_sem, late_own_sem,
     out_send_sem, out_recv_sem, out_own_sem,
 ):
     seq, res = lax.axis_index("seq"), lax.axis_index("res")
@@ -267,78 +270,158 @@
     grads[1] = rows_dot(score_grad, q_all[...], TN)
     grads[2] = rows_dot(prob_low, g_all[...], TN)
 
-    def place(k):
-        return (yh + near_first(3 - k)) % 4
-
-    def send_back(k, _):
-        src = place(k)
+    def unit(k):
+        return (yh + 2 - k // 2 + 2 * (k // 3)) % 4, (k + 3) // 4
+
+    def pack(src, h):
         for j in range(3):
-            for s in range(SEQ_RUN // 2):
+            for n in range(QUARTER):
+                lanes = (h * QUARTER + n) * 128
                 for r in range(RES):
                     rows = pl.ds(pl.multiple_of(src * 32 + r * 8, 8), 8)
-                    wide[pl.ds(j * HALF + s * RES + r, 8, stride=3 * HALF), :] = grads[
-                        j, rows, s * 128 : s * 128 + 128
+                    wide_back[pl.ds(j * PART + n * RES + r, 8, stride=3 * PART), :] = grads[
+                        j, rows, lanes : lanes + 128
                     ]
-        back_send[src] = wide[...].astype(BF16).reshape(8, 3 * HALF, 128)
-
-        def one(j, _):
-            to = (g + j) % 8
+        back_send[src, h] = wide_back[...].astype(BF16).reshape(8, 3 * PART, 128)
+
+    def send_back(src, h):
+        def one(k, _):
+            to = (g + k) % 8
             pltpu.make_async_remote_copy(
-                back_send.at[src, to], back_recv.at[src, g], back_send_sem, back_recv_sem.at[src],
+                back_send.at[src, h, to], back_recv.at[src, h, g],
+                back_send_sem.at[src, h], back_recv_sem.at[src, h],
                 device_id=head_peer(to), device_id_type=MESH,
             ).start()
             return 0
 
         lax.fori_loop(1, 8, one, 0)
-        pltpu.make_async_copy(back_send.at[src, g], back_recv.at[src, g], back_own_sem.at[src]).start()
-        return 0
-
-    lax.fori_loop(0, 4, send_back, 0)
-
-    low_back = lax.broadcasted_iota(jnp.int32, (3 * HALF, 128), 1) < HEAD_DIM
-
-    def out_copy(to, slot, n):
+        pltpu.make_async_copy(
+            back_send.at[src, h, g], back_recv.at[src, h, g], back_own_sem.at[src, h]
+        ).start()
+
+    def early_copy(to, slot):
         return pltpu.make_async_remote_copy(
-            out_send.at[to, n], out.at[run(slot), :, pl.ds(n * (D // 2), D // 2)], out_send_sem, out_recv_sem.at[slot, n],
+            back_send.at[to, 0], early.at[slot], early_send_sem.at[to], early_recv_sem.at[slot],
             device_id=y_peer(to), device_id_type=MESH,
         )
 
-    def finish(src, remote):
-        wait_bytes(back_recv.at[src, pl.ds(0, 7)], back_recv_sem.at[src])
-        pltpu.make_async_copy(back_send.at[src, g], back_recv.at[src, g], back_own_sem.at[src]).wait()
+    def send_early(k, _):
+        src = (yh + 1 + 2 * k) % 4
+        pack(src, 0)
+        early_copy(src, yh).start()
+        return 0
+
+    lax.fori_loop(0, 2, send_early, 0)
+    pack(far, 0)
+    send_back(far, 0)
+
+    def send_second(k, _):
+        src = unit(k)[0]
+        pack(src, 1)
+        send_back(src, 1)
+        return 0
+
+    lax.fori_loop(1, 4, send_second, 0)
+    pack(yh, 0)
+    send_back(yh, 0)
+    pack(yh, 1)
+    send_back(yh, 1)
+
+    low_back = lax.broadcasted_iota(jnp.int32, (3 * PART, 128), 1) < HEAD_DIM
+
+    def unfold(block):
         tops, bottoms = [], []
         for p in range(4):
-            a, b = back_recv[src, 2 * p], back_recv[src, 2 * p + 1]
+            a, b = block(2 * p), block(2 * p + 1)
             tops.append(jnp.where(low_back, a, b))
             bottoms.append(pltpu.roll(jnp.where(low_back, b, a), HEAD_DIM, 1))
         top, bottom = jnp.concatenate(tops, axis=1), jnp.concatenate(bottoms, axis=1)
-        sides = [
-            jnp.concatenate([top[j * HALF : (j + 1) * HALF], bottom[j * HALF : (j + 1) * HALF]], axis=0)
+        return [
+            jnp.concatenate([top[j * PART : (j + 1) * PART], bottom[j * PART : (j + 1) * PART]], axis=0)
             for j in range(3)
         ]
-        for n in range(2):
-            cols = slice(n * (D // 2), (n + 1) * (D // 2))
-            grad = None
-            for side, weight in zip(sides, (wq, wk, wv)):
-                term = rows_dot(side, weight[cols, :], NT)
-                grad = term if grad is None else grad + term
-            out_send[src, n] = grad.astype(BF16).reshape(SEQ_RUN, RES, D // 2)
-            if remote:
-                out_copy(src, yh, n).start()
-
-    def finish_far(k, _):
-        src = place(k)
-        finish(src, True)
-        return 0
-
-    lax.fori_loop(0, 3, finish_far, 0)
-    finish(yh, False)
-    own_outs = [
-        pltpu.make_async_copy(out_send.at[yh, n], out.at[run(yh), :, pl.ds(n * (D // 2), D // 2)], out_own_sem.at[n])
-        for n in range(2)
-    ]
-    for own_out in own_outs:
-        own_out.start()
+
+    def finish(sides, columns, keep):
+        grad = None
+        for side, weight in zip(sides, (wq, wk, wv)):
+            term = rows_dot(side, weight[columns * (D // 2) : (columns + 1) * (D // 2), :], NT)
+            grad = term if grad is None else grad + term
+        pieces = grad.astype(BF16).reshape(-1, 2, QUARTER, RES, D // 2)
+        for n in range(pieces.shape[0]):
+            out_send[keep + n, columns] = pieces[n]
+
+    def place(run_at, h, columns, piece):
+        start = pl.multiple_of(run_at * SEQ_RUN, SEQ_RUN) + h * QUARTER + piece * (SEQ_RUN // 2)
+        return out.at[pl.ds(start, QUARTER), :, pl.ds(columns * (D // 2), D // 2)]
+
+    def arrived(src, h):
+        wait_bytes(back_recv.at[src, h, pl.ds(0, 7)], back_recv_sem.at[src, h])
+        pltpu.make_async_copy(
+            back_send.at[src, h, g], back_recv.at[src, h, g], back_own_sem.at[src, h]
+        ).wait()
+        return unfold(lambda head: back_recv[src, h, head])
+
+    def finish_unit(k, _):
+        src, h = unit(k)
+        sides = arrived(src, h)
+        for columns in range(2):
+            finish(sides, columns, k)
+            for piece in range(2):
+                pltpu.make_async_remote_copy(
+                    out_send.at[k, columns, piece], place(yh, h, columns, piece),
+                    out_send_sem.at[k], out_recv_sem.at[yh],
+                    device_id=y_peer(src), device_id_type=MESH,
+                ).start()
+
+        @pl.when(k == 1)
+        def _():
+            def forward(n, _):
+                slot = (yh + 1 + 2 * n) % 4
+                early_copy(slot, slot).wait_recv()
+
+                def one(k, _):
+                    to = (g + k) % 8
+                    pltpu.make_async_remote_copy(
+                        early.at[slot, to], late.at[slot, g], late_send_sem.at[slot], late_recv_sem.at[slot],
+                        device_id=head_peer(to), device_id_type=MESH,
+                    ).start()
+                    return 0
+
+                lax.fori_loop(1, 8, one, 0)
+                pltpu.make_async_copy(early.at[slot, g], late.at[slot, g], late_own_sem.at[slot]).start()
+                return 0
+
+            lax.fori_loop(0, 2, forward, 0)
+
+        return 0
+
+    lax.fori_loop(0, 4, finish_unit, 0)
+
+    def both(one, two):
+        return [jnp.concatenate(pair, axis=0) for pair in zip(one, two)]
+
+    own_outs = []
+
+    def finish_here(sides, keep, runs):
+        for columns in range(2):
+            finish(sides, columns, keep)
+            for n, (run_at, h) in enumerate(runs):
+                for piece in range(2):
+                    copy = pltpu.make_async_copy(
+                        out_send.at[keep + n, columns, piece], place(run_at, h, columns, piece),
+                        out_own_sem.at[len(own_outs)],
+                    )
+                    copy.start()
+                    own_outs.append(copy)
+
+    finish_here(both(arrived(yh, 0), arrived(yh, 1)), 4, ((yh, 0), (yh, 1)))
+
+    def arrived_late(slot):
+        wait_bytes(late.at[slot, pl.ds(0, 7)], late_recv_sem.at[slot])
+        pltpu.make_async_copy(early.at[slot, g], late.at[slot, g], late_own_sem.at[slot]).wait()
+        return unfold(lambda head: late[slot, head])
+
+    finish_here(both(arrived_late(after), arrived_late(before)), 6, ((after, 0), (before, 0)))
 
     wait_bytes(g_own.at[pl.ds(0, 7)], near_send_sem)
     for to in (after, before, far):
@@ -348,16 +431,21 @@
     wait_bytes(part_recv.at[pl.ds(0, 7)], part_send_sem)
     wait_bytes(total_recv.at[pl.ds(0, 7)], total_send_sem)
     wait_bytes(probs.at[pl.ds(0, 7)], probs_send_sem)
-    wait_bytes(back_send.at[:, pl.ds(0, 7)], back_send_sem)
-    wait_bytes(out_send.at[pl.ds(0, 3)], out_send_sem)
-
-    def wait_out(k, _):
-        src = (yh + k) % 4
-        for n in range(2):
-            out_copy(src, src, n).wait_recv()
-        return 0
-
-    lax.fori_loop(1, 4, wait_out, 0)
+    def wait_back(k, _):
+        src, h = unit(k)
+        wait_bytes(back_send.at[src, h, pl.ds(0, 7)], back_send_sem.at[src, h])
+        wait_bytes(out_send.at[k], out_send_sem.at[k])
+        return 0
+
+    lax.fori_loop(0, 4, wait_back, 0)
+    for h in range(2):
+        wait_bytes(back_send.at[yh, h, pl.ds(0, 7)], back_send_sem.at[yh, h])
+    for slot in (after, before):
+        early_copy(slot, yh).wait_send()
+        wait_bytes(late.at[slot, pl.ds(0, 7)], late_send_sem.at[slot])
+    wait_bytes(out.at[pl.ds(0, SEQ_RUN)], out_recv_sem.at[far])
+    for slot in (after, before):
+        wait_bytes(out.at[pl.ds(0, SEQ_RUN // 2)], out_recv_sem.at[slot])
     for own_out in own_outs:
         own_out.wait()
 
@@ -397,14 +485,18 @@
             vmem((2, 16, 128), F32),
             vmem((8, 2, 16, 128), F32),
             vmem((8, 2, 16, 128), BF16),
-            vmem((4, 8, 3 * HALF, 128), BF16),
-            vmem((4, 8, 3 * HALF, 128), BF16),
-            vmem((4, 2, SEQ_RUN, RES, D // 2), BF16),
+            vmem((8 * 3 * PART, 128), F32),
+            vmem((4, 2, 8, 3 * PART, 128), BF16),
+            vmem((4, 2, 8, 3 * PART, 128), BF16),
+            vmem((4, 8, 3 * PART, 128), BF16),
+            vmem((4, 8, 3 * PART, 128), BF16),
+            vmem((8, 2, 2, QUARTER, RES, D // 2), BF16),
             dma((6,)), dma((4,)), dma((4,)), dma, dma, dma,
             dma, dma((4,)), dma, dma, dma((4,)), dma((4,)),
             dma, dma, dma, dma,
-            dma, dma, dma, dma((4,)), dma((4,)),
-            dma, dma((4, 2)), dma((2,)),
+            dma, dma, dma((4, 2)), dma((4, 2)), dma((4, 2)),
+            dma((4,)), dma((4,)), dma((4,)), dma((4,)), dma((4,)),
+            dma((4,)), dma((4,)), dma((16,)),
         ],
         compiler_params=pltpu.CompilerParams(
             collective_id=0, has_side_effects=True, vmem_limit_bytes=54784 * 2**10

time: 70.2 us -> 69.1 us (0.984)
  Pallas kernels: 69.4 us -> 68.2 us
    pallas_call x1, Pallas kernels: 69.4 us -> 68.2 us  [body(): pl.pallas_call(lambda *refs: kernel(scale, *refs), out_shape=jax.ShapeDty...]
where the time goes in v5:
time: 69.1 us; the launch traced here: 69 us
  Pallas kernels  68.2 us (99%)
  local copies, waits for them, and re-layouts  0.75 us (1%)
    pallas_call x1, Pallas kernels, body(): pl.pallas_call(lambda *refs: kernel(scale, *refs), out_shape=jax.ShapeDty...  68.2 us

profile of v5, /device:TPU:1, one launch (start us, length us, event | category | flops | bytes accessed | tf_op | source)
XLA Modules:
  0.0 69.0 jit_solution(6596620256199739429)
XLA Ops:
  0.0 68.2 %shard_map.64 = bf16[64,4,768]{2,1,0:T(4,128)(2,1)S(1)} custom-call(bf16[64,4,768]{2,1,0:T(4,128)(2,1)} %refs_0_.1, bf16[64,4,768]{2,1,0:T(4,128)(2,1)} %refs_1_.1, bf16[768,512]{1,0:T(8,128)(2,1)} %refs_2_.1, bf16[768,512]{1,0:T(8,128)(2,1)} %refs_3_.1, bf16[768,512]{1,0:T(8,128)(2,1)} %refs_4_.1, bf16[512,768]{1,0:T(8,128)(2,1)} %refs_5_.1), custom_call_target="tpu_custom_call" | custom-call | flops 2000000000 | bytes 5000000 | tf_op jit(solution)/shard_map/pallas_call | solution.py:459
  68.2 0.7 %copy.8 = bf16[64,4,768]{2,1,0:T(4,128)(2,1)} copy(bf16[64,4,768]{2,1,0:T(4,128)(2,1)S(1)} %shard_map.64) | data formatting | bytes 786432

commit v6 on v5

--- a/solution.py
+++ b/solution.py
@@ -205,13 +205,6 @@
     x_copy(far, far).wait_recv()
     do_qkv(far)
 
-    def next_qkv(k, _):
-        take_qkv((yh + near_first(k)) % 4)
-        return 0
-
-    lax.fori_loop(1, 4, next_qkv, 0)
-    part[:, 0] = rows_dot(q_all[...], k_all[...], NT).reshape(8, 16, 128)
-
     def next_g(k, _):
         src = (yh + near_first(k)) % 4
         g_copy(src, src).wait_recv()
@@ -219,36 +212,54 @@
         return 0
 
     lax.fori_loop(1, 4, next_g, 0)
-    part[:, 1] = rows_dot(g_all[...], v_all[...], NT).reshape(8, 16, 128)
-
-    def send_part(k, _):
-        to = (z + k) % 8
-        pltpu.make_async_remote_copy(
-            part.at[to], part_recv.at[z], part_send_sem, part_recv_sem,
-            device_id=z_peer(to), device_id_type=MESH,
-        ).start()
-        return 0
-
-    lax.fori_loop(1, 8, send_part, 0)
-    part_recv[z] = part[z]
-    wait_bytes(part_recv.at[pl.ds(0, 7)], part_recv_sem)
-    total[...] = jnp.sum(part_recv[...], axis=0)
-
-    def send_total(k, _):
-        to = (w + k) % 8
-        pltpu.make_async_remote_copy(
-            total, total_recv.at[w], total_send_sem, total_recv_sem,
-            device_id=line_peer(to), device_id_type=MESH,
-        ).start()
-        return 0
-
-    lax.fori_loop(1, 8, send_total, 0)
-    total_recv[w] = total[...]
-    wait_bytes(total_recv.at[pl.ds(0, 7)], total_recv_sem)
-    sums = jnp.sum(total_recv[...], axis=0)
-    scores, prob_grad = scale * sums[0], sums[1]
+
+    def next_qkv(k, _):
+        take_qkv((yh + near_first(k)) % 4)
+        return 0
+
+    lax.fori_loop(1, 4, next_qkv, 0)
+
+    def send_part(n, product):
+        part[n] = product.reshape(8, 16, 128)
+
+        def one(k, _):
+            to = (z + k) % 8
+            pltpu.make_async_remote_copy(
+                part.at[n, to], part_recv.at[n, z], part_send_sem.at[n], part_recv_sem.at[n],
+                device_id=z_peer(to), device_id_type=MESH,
+            ).start()
+            return 0
+
+        lax.fori_loop(1, 8, one, 0)
+        part_recv[n, z] = part[n, z]
+
+    def send_total(n):
+        wait_bytes(part_recv.at[n, pl.ds(0, 7)], part_recv_sem.at[n])
+        total[n] = jnp.sum(part_recv[n], axis=0)
+
+        def one(k, _):
+            to = (w + k) % 8
+            pltpu.make_async_remote_copy(
+                total.at[n], total_recv.at[n, w], total_send_sem.at[n], total_recv_sem.at[n],
+                device_id=line_peer(to), device_id_type=MESH,
+            ).start()
+            return 0
+
+        lax.fori_loop(1, 8, one, 0)
+        total_recv[n, w] = total[n]
+
+    def whole(n):
+        wait_bytes(total_recv.at[n, pl.ds(0, 7)], total_recv_sem.at[n])
+        return jnp.sum(total_recv[n], axis=0)
+
+    send_part(0, rows_dot(q_all[...], k_all[...], NT))
+    send_part(1, rows_dot(g_all[...], v_all[...], NT))
+    send_total(0)
+    send_total(1)
+    scores = scale * whole(0)
     grown = jnp.exp(scores - jnp.max(scores, axis=-1, keepdims=True))
     probability = grown / jnp.sum(grown, axis=-1, keepdims=True)
+    prob_grad = whole(1)
     row_total = jnp.sum(probability * prob_grad, axis=-1, keepdims=True)
     probs[z, 0] = (scale * probability * (prob_grad - row_total)).astype(BF16)
     probs[z, 1] = probability.astype(BF16)
@@ -428,8 +439,9 @@
         x_copy(to, yh).wait_send()
     wait_bytes(g_recv.at[pl.ds(0, 3)], g_send_sem)
     wait_bytes(qkv_send.at[:, pl.ds(0, 7)], qkv_send_sem)
-    wait_bytes(part_recv.at[pl.ds(0, 7)], part_send_sem)
-    wait_bytes(total_recv.at[pl.ds(0, 7)], total_send_sem)
+    for n in range(2):
+        wait_bytes(part_recv.at[n, pl.ds(0, 7)], part_send_sem.at[n])
+        wait_bytes(total_recv.at[n, pl.ds(0, 7)], total_send_sem.at[n])
     wait_bytes(probs.at[pl.ds(0, 7)], probs_send_sem)
     def wait_back(k, _):
         src, h = unit(k)
@@ -480,10 +492,10 @@
             vmem((128, SEQ_RUN * HEAD_DIM), BF16),
             vmem((128, SEQ_RUN * HEAD_DIM), BF16),
             vmem((3, 128, SEQ_RUN * HEAD_DIM), F32),
-            vmem((8, 2, 16, 128), F32),
-            vmem((8, 2, 16, 128), F32),
+            vmem((2, 8, 16, 128), F32),
+            vmem((2, 8, 16, 128), F32),
             vmem((2, 16, 128), F32),
-            vmem((8, 2, 16, 128), F32),
+            vmem((2, 8, 16, 128), F32),
             vmem((8, 2, 16, 128), BF16),
             vmem((8 * 3 * PART, 128), F32),
             vmem((4, 2, 8, 3 * PART, 128), BF16),
@@ -493,7 +505,7 @@
             vmem((8, 2, 2, QUARTER, RES, D // 2), BF16),
             dma((6,)), dma((4,)), dma((4,)), dma, dma, dma,
             dma, dma((4,)), dma, dma, dma((4,)), dma((4,)),
-            dma, dma, dma, dma,
+            dma((2,)), dma((2,)), dma((2,)), dma((2,)),
             dma, dma, dma((4, 2)), dma((4, 2)), dma((4, 2)),
             dma((4,)), dma((4,)), dma((4,)), dma((4,)), dma((4,)),
             dma((4,)), dma((4,)), dma((16,)),

time: 69.1 us -> 68 us (0.984)
  Pallas kernels: 68.2 us -> 67.1 us
    pallas_call x1, Pallas kernels: 68.2 us -> 67.1 us  [body(): pl.pallas_call(lambda *refs: kernel(scale, *refs), out_shape=jax.ShapeDty...]
where the time goes in v6:
time: 68 us; the launch traced here: 67.8 us
  Pallas kernels  67.1 us (99%)
  local copies, waits for them, and re-layouts  0.75 us (1%)
    pallas_call x1, Pallas kernels, body(): pl.pallas_call(lambda *refs: kernel(scale, *refs), out_shape=jax.ShapeDty...  67.1 us

profile of v6, /device:TPU:1, one launch (start us, length us, event | category | flops | bytes accessed | tf_op | source)
XLA Modules:
  0.0 67.8 jit_solution(8025331144781309924)
XLA Ops:
  0.0 67.1 %shard_map.64 = bf16[64,4,768]{2,1,0:T(4,128)(2,1)S(1)} custom-call(bf16[64,4,768]{2,1,0:T(4,128)(2,1)} %refs_0_.1, bf16[64,4,768]{2,1,0:T(4,128)(2,1)} %refs_1_.1, bf16[768,512]{1,0:T(8,128)(2,1)} %refs_2_.1, bf16[768,512]{1,0:T(8,128)(2,1)} %refs_3_.1, bf16[768,512]{1,0:T(8,128)(2,1)} %refs_4_.1, bf16[512,768]{1,0:T(8,128)(2,1)} %refs_5_.1), custom_call_target="tpu_custom_call" | custom-call | flops 2000000000 | bytes 5000000 | tf_op jit(solution)/shard_map/pallas_call | solution.py:471
  67.1 0.7 %copy.8 = bf16[64,4,768]{2,1,0:T(4,128)(2,1)} copy(bf16[64,4,768]{2,1,0:T(4,128)(2,1)S(1)} %shard_map.64) | data formatting | bytes 786432

commit v7 on v6

--- a/solution.py
+++ b/solution.py
@@ -259,27 +259,29 @@
     scores = scale * whole(0)
     grown = jnp.exp(scores - jnp.max(scores, axis=-1, keepdims=True))
     probability = grown / jnp.sum(grown, axis=-1, keepdims=True)
+    def send_probs(n):
+        def one(k, _):
+            to = (z + k) % 8
+            pltpu.make_async_remote_copy(
+                probs.at[n, z], probs.at[n, z], probs_send_sem.at[n], probs_recv_sem.at[n],
+                device_id=z_peer(to), device_id_type=MESH,
+            ).start()
+            return 0
+
+        lax.fori_loop(1, 8, one, 0)
+
+    probs[1, z] = probability.astype(BF16)
+    send_probs(1)
     prob_grad = whole(1)
     row_total = jnp.sum(probability * prob_grad, axis=-1, keepdims=True)
-    probs[z, 0] = (scale * probability * (prob_grad - row_total)).astype(BF16)
-    probs[z, 1] = probability.astype(BF16)
-
-    def send_probs(k, _):
-        to = (z + k) % 8
-        pltpu.make_async_remote_copy(
-            probs.at[z], probs.at[z], probs_send_sem, probs_recv_sem,
-            device_id=z_peer(to), device_id_type=MESH,
-        ).start()
-        return 0
-
-    lax.fori_loop(1, 8, send_probs, 0)
-    wait_bytes(probs.at[pl.ds(0, 7)], probs_recv_sem)
-    score_grad = probs[:, 0].reshape(128, 128)
-    prob_low = probs[:, 1].reshape(128, 128)
-
+    probs[0, z] = (scale * probability * (prob_grad - row_total)).astype(BF16)
+    send_probs(0)
+    wait_bytes(probs.at[1, pl.ds(0, 7)], probs_recv_sem.at[1])
+    grads[2] = rows_dot(probs[1].reshape(128, 128), g_all[...], TN)
+    wait_bytes(probs.at[0, pl.ds(0, 7)], probs_recv_sem.at[0])
+    score_grad = probs[0].reshape(128, 128)
     grads[0] = rows_dot(score_grad, k_all[...])
     grads[1] = rows_dot(score_grad, q_all[...], TN)
-    grads[2] = rows_dot(prob_low, g_all[...], TN)
 
     def unit(k):
         return (yh + 2 - k // 2 + 2 * (k // 3)) % 4, (k + 3) // 4
@@ -442,7 +444,8 @@
     for n in range(2):
         wait_bytes(part_recv.at[n, pl.ds(0, 7)], part_send_sem.at[n])
         wait_bytes(total_recv.at[n, pl.ds(0, 7)], total_send_sem.at[n])
-    wait_bytes(probs.at[pl.ds(0, 7)], probs_send_sem)
+    for n in range(2):
+        wait_bytes(probs.at[n, pl.ds(0, 7)], probs_send_sem.at[n])
     def wait_back(k, _):
         src, h = unit(k)
         wait_bytes(back_send.at[src, h, pl.ds(0, 7)], back_send_sem.at[src, h])
@@ -496,7 +499,7 @@
             vmem((2, 8, 16, 128), F32),
             vmem((2, 16, 128), F32),
             vmem((2, 8, 16, 128), F32),
-            vmem((8, 2, 16, 128), BF16),
+            vmem((2, 8, 16, 128), BF16),
             vmem((8 * 3 * PART, 128), F32),
             vmem((4, 2, 8, 3 * PART, 128), BF16),
             vmem((4, 2, 8, 3 * PART, 128), BF16),
@@ -506,7 +509,7 @@
             dma((6,)), dma((4,)), dma((4,)), dma, dma, dma,
             dma, dma((4,)), dma, dma, dma((4,)), dma((4,)),
             dma((2,)), dma((2,)), dma((2,)), dma((2,)),
-            dma, dma, dma((4, 2)), dma((4, 2)), dma((4, 2)),
+            dma((2,)), dma((2,)), dma((4, 2)), dma((4, 2)), dma((4, 2)),
             dma((4,)), dma((4,)), dma((4,)), dma((4,)), dma((4,)),
             dma((4,)), dma((4,)), dma((16,)),
         ],

time: 68 us -> 67.6 us (level)
  no operation moved by 1% of the time
where the time goes in v7:
time: 67.6 us; the launch traced here: 67.5 us
  Pallas kernels  66.7 us (99%)
  local copies, waits for them, and re-layouts  0.75 us (1%)
    pallas_call x1, Pallas kernels, body(): pl.pallas_call(lambda *refs: kernel(scale, *refs), out_shape=jax.ShapeDty...  66.7 us

profile of v7, /device:TPU:1, one launch (start us, length us, event | category | flops | bytes accessed | tf_op | source)
XLA Modules:
  0.0 67.5 jit_solution(2454855235401641283)
XLA Ops:
  0.0 66.7 %shard_map.64 = bf16[64,4,768]{2,1,0:T(4,128)(2,1)S(1)} custom-call(bf16[64,4,768]{2,1,0:T(4,128)(2,1)} %refs_0_.1, bf16[64,4,768]{2,1,0:T(4,128)(2,1)} %refs_1_.1, bf16[768,512]{1,0:T(8,128)(2,1)} %refs_2_.1, bf16[768,512]{1,0:T(8,128)(2,1)} %refs_3_.1, bf16[768,512]{1,0:T(8,128)(2,1)} %refs_4_.1, bf16[512,768]{1,0:T(8,128)(2,1)} %refs_5_.1), custom_call_target="tpu_custom_call" | custom-call | flops 2000000000 | bytes 5000000 | tf_op jit(solution)/shard_map/pallas_call | solution.py:474
  66.7 0.7 %copy.8 = bf16[64,4,768]{2,1,0:T(4,128)(2,1)} copy(bf16[64,4,768]{2,1,0:T(4,128)(2,1)S(1)} %shard_map.64) | data formatting | bytes 786432

commit v8 on v7

--- a/solution.py
+++ b/solution.py
@@ -357,15 +357,15 @@
     def finish(sides, columns, keep):
         grad = None
         for side, weight in zip(sides, (wq, wk, wv)):
-            term = rows_dot(side, weight[columns * (D // 2) : (columns + 1) * (D // 2), :], NT)
+            term = rows_dot(side, weight[...], NT)
             grad = term if grad is None else grad + term
-        pieces = grad.astype(BF16).reshape(-1, 2, QUARTER, RES, D // 2)
+        pieces = grad.astype(BF16).reshape(-1, 2, QUARTER, RES, D)
         for n in range(pieces.shape[0]):
             out_send[keep + n, columns] = pieces[n]
 
     def place(run_at, h, columns, piece):
         start = pl.multiple_of(run_at * SEQ_RUN, SEQ_RUN) + h * QUARTER + piece * (SEQ_RUN // 2)
-        return out.at[pl.ds(start, QUARTER), :, pl.ds(columns * (D // 2), D // 2)]
+        return out.at[pl.ds(start, QUARTER)]
 
     def arrived(src, h):
         wait_bytes(back_recv.at[src, h, pl.ds(0, 7)], back_recv_sem.at[src, h])
@@ -377,7 +377,7 @@
     def finish_unit(k, _):
         src, h = unit(k)
         sides = arrived(src, h)
-        for columns in range(2):
+        for columns in range(1):
             finish(sides, columns, k)
             for piece in range(2):
                 pltpu.make_async_remote_copy(
@@ -416,7 +416,7 @@
     own_outs = []
 
     def finish_here(sides, keep, runs):
-        for columns in range(2):
+        for columns in range(1):
             finish(sides, columns, keep)
             for n, (run_at, h) in enumerate(runs):
                 for piece in range(2):
@@ -505,7 +505,7 @@
             vmem((4, 2, 8, 3 * PART, 128), BF16),
             vmem((4, 8, 3 * PART, 128), BF16),
             vmem((4, 8, 3 * PART, 128), BF16),
-            vmem((8, 2, 2, QUARTER, RES, D // 2), BF16),
+            vmem((8, 1, 2, QUARTER, RES, D), BF16),
             dma((6,)), dma((4,)), dma((4,)), dma, dma, dma,
             dma, dma((4,)), dma, dma, dma((4,)), dma((4,)),
             dma((2,)), dma((2,)), dma((2,)), dma((2,)),

time: 67.6 us -> 67.1 us (level)
  no operation moved by 1% of the time
where the time goes in v8:
time: 67.1 us; the launch traced here: 66.9 us
  Pallas kernels  66.2 us (99%)
  local copies, waits for them, and re-layouts  0.75 us (1%)
    pallas_call x1, Pallas kernels, body(): pl.pallas_call(lambda *refs: kernel(scale, *refs), out_shape=jax.ShapeDty...  66.2 us

profile of v8, /device:TPU:1, one launch (start us, length us, event | category | flops | bytes accessed | tf_op | source)
XLA Modules:
  0.0 66.9 jit_solution(4575004842959811429)
XLA Ops:
  0.0 66.2 %shard_map.64 = bf16[64,4,768]{2,1,0:T(4,128)(2,1)S(1)} custom-call(bf16[64,4,768]{2,1,0:T(4,128)(2,1)} %refs_0_.1, bf16[64,4,768]{2,1,0:T(4,128)(2,1)} %refs_1_.1, bf16[768,512]{1,0:T(8,128)(2,1)} %refs_2_.1, bf16[768,512]{1,0:T(8,128)(2,1)} %refs_3_.1, bf16[768,512]{1,0:T(8,128)(2,1)} %refs_4_.1, bf16[512,768]{1,0:T(8,128)(2,1)} %refs_5_.1), custom_call_target="tpu_custom_call" | custom-call | flops 2000000000 | bytes 5000000 | tf_op jit(solution)/shard_map/pallas_call | solution.py:474
  66.2 0.7 %copy.8 = bf16[64,4,768]{2,1,0:T(4,128)(2,1)} copy(bf16[64,4,768]{2,1,0:T(4,128)(2,1)S(1)} %shard_map.64) | data formatting | bytes 786432
